TPU v7x, 32 devices: a whole 2x2x4 slice. The times are simulated.
32 devices in a mesh: face: 2 (over core), sub: 16 (over z, y, x).
Axes of the slice: x: 2, y: 2, z: 4, core: 2. Of those that a mesh axis runs over, the one named last changes fastest.
Arguments:
- features: bfloat16 [768, 24, 192], P(('face', 'sub')), may hold values from -6 to 6
- w_first: bfloat16 [3, 3, 192, 192], replicated, may hold values from -0.15625 to 0.15625
- b_first: float32 [192], replicated, may hold values from -3 to 3
- w_second: bfloat16 [3, 3, 192, 192], replicated, may hold values from -0.15625 to 0.15625
- neighbours: int32 [32, 4], replicated, may hold values from 0 to 31, as said below
- rotations: int32 [32, 4], replicated, may hold values from 0 to 3
- cotangent: bfloat16 [384, 12, 192], P(('face', 'sub')), may hold values from -6 to 6
Outputs:
- pooled: bfloat16 [384, 12, 192], P(('face', 'sub'))
- grad_input: bfloat16 [768, 24, 192], P(('face', 'sub'))
- grad_w1: float32 [3, 3, 192, 192], replicated
- grad_b1: float32 [192], replicated
- grad_w2: float32 [3, 3, 192, 192], replicated
Inputs may be any that keep to these rules, and one draw needn't show every extreme that they name: neighbours[d, e] is a tile f * 16 + s other than d; it has the same f as d or the same s as d; two tiles of the same f share at most one edge, and no tile names the same tile of its own f at two edges.
All inputs are finite; a program needn't handle non-finite values.
Results may differ from a plain program's by a relative error of at most 0.012.
Values may be sent and summed in bfloat16 or wider, within the bound.
A program may use at most 64 MiB of HBM per device.

v0:
```python
import functools
import math

import jax
import jax.numpy as jnp
from jax import lax
from jax.experimental import pallas as pl
from jax.experimental.pallas import tpu as pltpu
from jax.sharding import PartitionSpec as P

LANES = 128
W = 32
F32, BF16 = jnp.float32, jnp.bfloat16
MESH = pl.DeviceIdType.MESH


def iota(shape, dim):
    return lax.broadcasted_iota(jnp.int32, shape, dim)


def hot(mask):
    return jnp.where(mask, 1.0, 0.0).astype(BF16)


def dot(a, b, ca=1, cb=0):
    return lax.dot_general(a, b, (((ca,), (cb,)), ((), ())), preferred_element_type=F32)


def split(x):
    hi = x.astype(BF16)
    return hi, (x - hi.astype(F32)).astype(BF16)


def rim_pos(q, extent, pad):
    e, p = q >> 5, (q & (W - 1)) + pad
    far = extent - 1 + 2 * pad
    pos = jnp.where(e == 0, p, jnp.where(e == 1, p * W + far, jnp.where(e == 2, far * W + p, p * W)))
    return jnp.where((q & (W - 1)) < extent, pos, -1)


def pool_pos(r):
    return ((r >> 6) << 4) + ((r & (W - 1)) >> 1)


def kernel(S, F, chunk, scale, nbr, rot, feat, cot, w1, b1, w2,
           pooled, gin, gath,
           send_mat, recv_mat, pad_in, pad_act, gpad1, gpad2, cotp,
           win_in, win_act, gs1, gs2, hidden, second, pg, gact,
           ex_out, ex_in, wf, wb, w1in, red, accf, w2in, red2, acc2, w3in,
           ex_ss, ex_rs, w_ss, w_rs):
    T, C = feat.shape[0], feat.shape[2]
    H = T // 2
    face, sub = lax.axis_index("face"), lax.axis_index("sub")
    me = face * S + sub
    part = chunk * S
    A = 4 if S % 4 == 0 else 1
    B = S // A
    a_id, b_id = sub // B, lax.rem(sub, B)
    group = chunk * A
    M, MP = T * W, (T + 2) * W

    def peers(count, mine, body):
        def step(d, c):
            body(lax.rem(mine + d, count))
            return c
        lax.fori_loop(1, count, step, 0)

    barrier = pltpu.get_barrier_semaphore()
    peers(S, sub, lambda j: pl.semaphore_signal(barrier, inc=1, device_id=(face, j), device_id_type=MESH))
    peers(F, face, lambda f: pl.semaphore_signal(barrier, inc=1, device_id=(f, sub), device_id_type=MESH))

    p32 = iota((W, 4 * W), 0)
    c32 = iota((W, 4 * W), 1)

    def put_slot(k, hit, src, flip, edge):
        tgt = jnp.where(flip == 1, src * W + T - 1 - p32, src * W + p32)
        base = pl.multiple_of(k * W, W)
        send_mat[pl.ds(base, W), :] = hot((c32 == tgt) & (p32 < T) & (hit == 1))
        recv_mat[pl.ds(base, W), :] = hot((c32 == edge * W + p32) & (p32 < T) & (edge >= 0))

    def edge_code(tile, e):
        r = rot[tile, e]
        x = (e + 2) % 4
        src = (x + r) & 3
        odd = x % 2
        flip = jnp.where(r == 2, 1, jnp.where(r == 1, odd, jnp.where(r == 3, 1 - odd, 0)))
        return nbr[tile, e] == me, src, flip

    def in_face(j, c):
        hit, src, flip, edge = jnp.int32(0), jnp.int32(0), jnp.int32(0), jnp.int32(-1)
        for e in range(4):
            h, s, f = edge_code(face * S + j, e)
            hit = jnp.where(h, 1, hit)
            src = jnp.where(h, s, src)
            flip = jnp.where(h, f, flip)
            edge = jnp.where(nbr[me, e] == face * S + j, e, edge)
        put_slot(j, hit, src, flip, edge)
        return c

    lax.fori_loop(0, S, in_face, 0)

    def cross(f, c):
        for e in range(4):
            h, s, fl = edge_code(f * S + sub, e)
            other = f != face
            hit = jnp.where(h & other, 1, 0)
            edge = jnp.where((nbr[me, e] == f * S + sub) & other, e, -1)
            put_slot(S + f * 4 + e, hit, s, fl, edge)
        return c

    lax.fori_loop(0, F, cross, 0)

    for ph in range(4):
        ex_in[ph, pl.ds(pl.multiple_of(sub * W, W), W), :] = jnp.zeros((W, C), BF16)
        ex_in[ph, pl.ds(pl.multiple_of((S + 4 * face) * W, W), 4 * W), :] = jnp.zeros((4 * W, C), BF16)

    def ex_sub(ph, j, s_in, r_idx):
        return pltpu.make_async_remote_copy(
            src_ref=ex_out.at[ph, pl.ds(pl.multiple_of(j * W, W), W), :],
            dst_ref=ex_in.at[ph, pl.ds(pl.multiple_of(s_in * W, W), W), :],
            send_sem=ex_ss.at[ph, j], recv_sem=ex_rs.at[ph, r_idx],
            device_id=(face, j), device_id_type=MESH)

    def ex_face(ph, f, f_in):
        return pltpu.make_async_remote_copy(
            src_ref=ex_out.at[ph, pl.ds(pl.multiple_of((S + 4 * f) * W, W), 4 * W), :],
            dst_ref=ex_in.at[ph, pl.ds(pl.multiple_of((S + 4 * f_in) * W, W), 4 * W), :],
            send_sem=ex_ss.at[ph, S + f], recv_sem=ex_rs.at[ph, S + f_in],
            device_id=(f, sub), device_id_type=MESH)

    def ex_start(ph, mat, rims):
        ex_out[ph] = dot(mat[...], rims).astype(BF16)
        peers(S, sub, lambda j: ex_sub(ph, j, sub, sub).start())
        peers(F, face, lambda f: ex_face(ph, f, face).start())

    def ex_wait(ph, mat):
        peers(S, sub, lambda j: ex_sub(ph, j, j, j).wait_recv())
        peers(F, face, lambda f: ex_face(ph, f, f).wait_recv())
        return dot(mat[...], ex_in[ph], 0, 0)

    def ex_drain(ph):
        peers(S, sub, lambda j: ex_sub(ph, j, sub, sub).wait_send())
        peers(F, face, lambda f: ex_face(ph, f, face).wait_send())

    own_rims = hot(iota((4 * W, M), 1) == rim_pos(iota((4 * W, 1), 0), T, 0))
    pad_rims = hot(iota((4 * W, MP), 1) == rim_pos(iota((4 * W, 1), 0), T, 1))
    own_place = hot(iota((M, 4 * W), 0) == rim_pos(iota((1, 4 * W), 1), T, 0))
    pad_place = hot(iota((MP, 4 * W), 0) == rim_pos(iota((1, 4 * W), 1), T, 1))

    def windows(src, dst, rows):
        for b in range(3):
            dst[b] = src[:, b:b + W, :].reshape(rows * W, C).astype(BF16)

    def add_halo(padded, halo):
        placed = dot(pad_place, halo.astype(BF16)).reshape(T + 2, W, C)
        padded[:, 0:W, :] = padded[:, 0:W, :] + placed

    def conv(win, wt, out, rows, back):
        half = rows

        def step(i, c):
            acc = None
            for a in range(3):
                for b in range(3):
                    off = pl.multiple_of(i * half, 16) + a * W
                    x = win[b, pl.ds(pl.multiple_of(off, 16), half), :]
                    tap = (2 - a) * 3 + 2 - b if back else a * 3 + b
                    d = dot(x, wt[tap * C:(tap + 1) * C, :], 1, 1 if back else 0)
                    acc = d if acc is None else acc + d
            out[pl.ds(pl.multiple_of(i * half, 16), half), :] = acc
            return c

        lax.fori_loop(0, 1, step, 0)

    def put(k, r, v):
        wf[k, r:r + v.shape[0], :] = v
        wb[k, r:r + v.shape[0], :] = v.astype(BF16)

    def weight_grad(k, win, gs):
        odd = None
        for t in range(9):
            a, b = t // 3, t % 3
            v = dot(win[b], gs[2, (2 - a) * W:(2 - a) * W + MP, :], 0, 0)
            put(k, t * C, v[:, 0:LANES])
            rest = v[:, LANES:C]
            if t % 2 == 0:
                odd = rest
            if t % 2 == 1 or t == 8:
                pair = jnp.concatenate([odd, rest], axis=1)
                put(k, (9 + t // 2) * C, pair)

    pad_in[...] = jnp.zeros(pad_in.shape, F32)
    pad_in[1:T + 1, 1:T + 1, :] = feat[...].astype(F32)
    flat_in = pad_in[1:T + 1, 1:W + 1, :].reshape(M, C)
    rims = dot(own_rims, flat_in.astype(BF16)).astype(BF16)
    pl.semaphore_wait(barrier, S + F - 2)
    ex_start(0, send_mat, rims)

    cotp[...] = jnp.zeros(cotp.shape, F32)
    cotp[:, 0:H, :] = cot[...].astype(F32)
    spread = hot(pool_pos(iota((M, 1), 0)) == iota((M, H * 16), 1))
    up = dot(spread, cotp[...].reshape(H * 16, C).astype(BF16)) * 0.25
    gpad2[...] = jnp.zeros(gpad2.shape, F32)
    gpad2[2:T + 2, 2:T + 2, :] = up.reshape(T, W, C)[:, 0:T, :]
    windows(gpad2, gs2, T + 4)
    conv(gs2, w2, pg, MP, True)
    rims = dot(pad_rims, pg[...].astype(BF16)).astype(BF16)
    ex_start(2, recv_mat, rims)
    gact[...] = pg[...].reshape(T + 2, W, C)[1:T + 1]
    pad_act[...] = jnp.zeros(pad_act.shape, F32)
    gpad1[...] = jnp.zeros(gpad1.shape, F32)

    add_halo(pad_in, ex_wait(0, recv_mat))
    windows(pad_in, win_in, T + 2)
    conv(win_in, w1, hidden, M, False)
    hid = hidden[...] + b1[...]
    sig = 1.0 / (1.0 + jnp.exp(-hid))
    act = (hid * sig).astype(BF16)
    rims = dot(own_rims, act).astype(BF16)
    ex_start(1, send_mat, rims)
    pad_act[1:T + 1, 1:T + 1, :] = act.astype(F32).reshape(T, W, C)[:, 0:T, :]

    def fold(middle, arrived):
        hi, lo = split(arrived)
        back = dot(own_place, hi) + dot(own_place, lo)
        return middle[:, 1:T + 1, :] + back.reshape(T, W, C)[:, 0:T, :]

    ga = fold(gact, ex_wait(2, send_mat)).astype(BF16).astype(F32)
    slope = (sig * (1.0 + hid * (1.0 - sig))).reshape(T, W, C)[:, 0:T, :]
    gh = (ga * slope).astype(BF16).astype(F32)
    gpad1[2:T + 2, 2:T + 2, :] = gh
    windows(gpad1, gs1, T + 4)

    rows = wf.shape[1]

    def face_copy(k, st, f, f_in):
        return pltpu.make_async_remote_copy(
            src_ref=wb.at[k, pl.ds(pl.multiple_of(f * part, 16), part), :],
            dst_ref=w1in.at[k, f_in],
            send_sem=w_ss.at[k, 0, f], recv_sem=w_rs.at[k, 0, f_in],
            device_id=(f, sub), device_id_type=MESH)

    def b_copy(k, j, j_in):
        return pltpu.make_async_remote_copy(
            src_ref=red.at[k, pl.ds(pl.multiple_of(j * group, 16), group), :],
            dst_ref=w2in.at[k, j_in],
            send_sem=w_ss.at[k, 1, j], recv_sem=w_rs.at[k, 1, j_in],
            device_id=(face, a_id * B + j), device_id_type=MESH)

    def a_copy(k, j, j_in):
        return pltpu.make_async_remote_copy(
            src_ref=red2.at[k, pl.ds(pl.multiple_of(j * chunk, 16), chunk), :],
            dst_ref=w3in.at[k, j_in],
            send_sem=w_ss.at[k, 2, j], recv_sem=w_rs.at[k, 2, j_in],
            device_id=(face, j * B + b_id), device_id_type=MESH)

    def spot(k, start, size):
        return gath.at[k, pl.ds(pl.multiple_of(start, 16), size), :]

    def a_gather(k, j, own):
        place = spot(k, face * part + b_id * group + own * chunk, chunk)
        return pltpu.make_async_remote_copy(
            src_ref=place, dst_ref=place,
            send_sem=w_ss.at[k, 3, j], recv_sem=w_rs.at[k, 3, own],
            device_id=(face, j * B + b_id), device_id_type=MESH)

    def b_gather(k, j, own):
        place = spot(k, face * part + own * group, group)
        return pltpu.make_async_remote_copy(
            src_ref=place, dst_ref=place,
            send_sem=w_ss.at[k, 4, j], recv_sem=w_rs.at[k, 4, own],
            device_id=(face, a_id * B + j), device_id_type=MESH)

    def face_gather(k, f, own):
        place = spot(k, own * part, part)
        return pltpu.make_async_remote_copy(
            src_ref=place, dst_ref=place,
            send_sem=w_ss.at[k, 5, f], recv_sem=w_rs.at[k, 5, own],
            device_id=(f, sub), device_id_type=MESH)

    def reduce_start(k):
        peers(F, face, lambda f: face_copy(k, 0, f, face).start())

    def summed(first, count, mine, ref, k):
        def step(d, tot):
            return tot + ref[k, lax.rem(mine + d, count)].astype(F32)
        return lax.fori_loop(1, count, step, first)

    def reduce_b(k):
        peers(F, face, lambda f: face_copy(k, 0, f, f).wait_recv())
        for r in range(B):
            at = pl.ds(pl.multiple_of(face * part + r * group, 16), group)
            tot = wf[k, at, :]
            for f in range(1, F):
                tot = tot + w1in[k, lax.rem(face + f, F), r * group:(r + 1) * group, :].astype(F32)
            accf[k, r * group:(r + 1) * group, :] = tot
            red[k, r * group:(r + 1) * group, :] = tot.astype(BF16)
        peers(B, b_id, lambda j: b_copy(k, j, b_id).start())

    def reduce_a(k):
        peers(B, b_id, lambda j: b_copy(k, j, j).wait_recv())
        tot = summed(accf[k, pl.ds(pl.multiple_of(b_id * group, 16), group), :], B, b_id, w2in, k)
        acc2[k] = tot
        red2[k] = tot.astype(BF16)
        peers(A, a_id, lambda j: a_copy(k, j, a_id).start())

    def gather_a(k):
        peers(A, a_id, lambda j: a_copy(k, j, j).wait_recv())
        tot = summed(acc2[k, pl.ds(pl.multiple_of(a_id * chunk, 16), chunk), :], A, a_id, w3in, k)
        own = pl.ds(pl.multiple_of(face * part + b_id * group + a_id * chunk, 16), chunk)
        gath[k, own, :] = (tot * scale).astype(BF16)
        peers(A, a_id, lambda j: a_gather(k, j, a_id).start())

    def gather_b(k):
        peers(A, a_id, lambda j: a_gather(k, j, j).wait_recv())
        peers(B, b_id, lambda j: b_gather(k, j, b_id).start())

    def gather_face(k):
        peers(B, b_id, lambda j: b_gather(k, j, j).wait_recv())
        peers(F, face, lambda f: face_gather(k, f, face).start())

    def gather_end(k):
        peers(F, face, lambda f: face_gather(k, f, f).wait_recv())

    def drain(k):
        peers(F, face, lambda f: face_copy(k, 0, f, face).wait_send())
        peers(B, b_id, lambda j: b_copy(k, j, b_id).wait_send())
        peers(A, a_id, lambda j: a_copy(k, j, a_id).wait_send())
        peers(A, a_id, lambda j: a_gather(k, j, a_id).wait_send())
        peers(B, b_id, lambda j: b_gather(k, j, b_id).wait_send())
        peers(F, face, lambda f: face_gather(k, f, face).wait_send())

    for k in range(2):
        put(k, 14 * C, jnp.zeros((rows - 14 * C, LANES), F32))
    weight_grad(0, win_in, gs1)
    bias = jnp.sum(jnp.sum(gh, axis=0), axis=0, keepdims=True)
    bias = jnp.concatenate([bias, jnp.zeros((1, 2 * LANES - C), F32)], axis=1)
    line = iota((16, LANES), 0)
    put(0, 14 * C, jnp.where(line == 0, bias[:, 0:LANES], jnp.where(line == 1, bias[:, LANES:], 0.0)))
    reduce_start(0)

    add_halo(pad_act, ex_wait(1, recv_mat))
    windows(pad_act, win_act, T + 2)
    reduce_b(0)
    weight_grad(1, win_act, gs2)
    reduce_start(1)
    conv(gs1, w1, pg, MP, True)
    rims = dot(pad_rims, pg[...].astype(BF16)).astype(BF16)
    ex_start(3, recv_mat, rims)
    reduce_a(0)
    reduce_b(1)
    conv(win_act, w2, second, M, False)
    gather_a(0)
    hi, lo = split(second[...] + pad_in[1:T + 1, 1:W + 1, :].reshape(M, C))
    mean = hot(pool_pos(iota((1, M), 1)) == iota((H * 16, M), 0))
    down = (dot(mean, hi) + dot(mean, lo)) * 0.25
    pooled[...] = down.reshape(H, 16, C)[:, 0:H, :].astype(BF16)
    reduce_a(1)
    gather_b(0)
    gact[...] = pg[...].reshape(T + 2, W, C)[1:T + 1]
    total = fold(gact, ex_wait(3, send_mat)) + gpad2[2:T + 2, 2:T + 2, :]
    gin[...] = total.astype(BF16)
    gather_a(1)
    gather_face(0)
    gather_b(1)
    gather_end(0)
    gather_face(1)
    gather_end(1)
    for ph in range(4):
        ex_drain(ph)
    for k in range(2):
        drain(k)


def finish(C, pooled_in, gin_in, gath, pooled, gin, gw1, gb1, gw2):
    pooled[...] = pooled_in[...]
    gin[...] = gin_in[...]
    for k, out in ((0, gw1), (1, gw2)):
        for t in range(9):
            left = gath[k, t * C:(t + 1) * C, :].astype(F32)
            pair = gath[k, (9 + t // 2) * C:(10 + t // 2) * C, :].astype(F32)
            half = C - LANES
            right = pair[:, 0:half] if t % 2 == 0 else pair[:, half:2 * half]
            out[t // 3, t % 3, :, 0:LANES] = left
            out[t // 3, t % 3, :, LANES:C] = right
    bias = gath[0, 14 * C:14 * C + 16, :].astype(F32)
    gb1[:, 0:LANES] = bias[0:1]
    gb1[:, LANES:C] = bias[1:2, 0:C - LANES]


def local(S, F, features, w_first, b_first, w_second, neighbours, rotations, cotangent):
    T, C = features.shape[1], features.shape[2]
    H = T // 2
    D = neighbours.shape[0]
    chunk = -(-(14 * C + 16) // (16 * D)) * 16
    A = 4 if S % 4 == 0 else 1
    B = S // A
    rows, part = chunk * D, chunk * S
    K = (S + 4 * F) * W
    scale = 1.0 / math.sqrt(D * T * T)
    vm = pl.BlockSpec(memory_space=pltpu.VMEM)
    sm = pl.BlockSpec(memory_space=pltpu.SMEM)
    n = max(S, F)
    pooled, gin, gath = pl.pallas_call(
        functools.partial(kernel, S, F, chunk, scale),
        out_shape=(
            jax.ShapeDtypeStruct((H, H, C), BF16),
            jax.ShapeDtypeStruct((T, T, C), BF16),
            jax.ShapeDtypeStruct((2, rows, LANES), BF16),
        ),
        in_specs=[sm, sm, vm, vm, vm, vm, vm],
        out_specs=(vm,) * 3,
        scratch_shapes=[
            pltpu.VMEM((K, 4 * W), BF16),
            pltpu.VMEM((K, 4 * W), BF16),
            pltpu.VMEM((T + 2, W + 8, C), F32),
            pltpu.VMEM((T + 2, W + 8, C), F32),
            pltpu.VMEM((T + 4, W + 8, C), F32),
            pltpu.VMEM((T + 4, W + 8, C), F32),
            pltpu.VMEM((H, 16, C), F32),
            pltpu.VMEM((3, (T + 2) * W, C), BF16),
            pltpu.VMEM((3, (T + 2) * W, C), BF16),
            pltpu.VMEM((3, (T + 4) * W, C), BF16),
            pltpu.VMEM((3, (T + 4) * W, C), BF16),
            pltpu.VMEM((T * W, C), F32),
            pltpu.VMEM((T * W, C), F32),
            pltpu.VMEM(((T + 2) * W, C), F32),
            pltpu.VMEM((T, W, C), F32),
            pltpu.VMEM((4, K, C), BF16),
            pltpu.VMEM((4, K, C), BF16),
            pltpu.VMEM((2, rows, LANES), F32),
            pltpu.VMEM((2, rows, LANES), BF16),
            pltpu.VMEM((2, F, part, LANES), BF16),
            pltpu.VMEM((2, part, LANES), BF16),
            pltpu.VMEM((2, part, LANES), F32),
            pltpu.VMEM((2, B, A * chunk, LANES), BF16),
            pltpu.VMEM((2, A * chunk, LANES), BF16),
            pltpu.VMEM((2, A * chunk, LANES), F32),
            pltpu.VMEM((2, A, chunk, LANES), BF16),
            pltpu.SemaphoreType.DMA((4, S + F)),
            pltpu.SemaphoreType.DMA((4, S + F)),
            pltpu.SemaphoreType.DMA((2, 6, n)),
            pltpu.SemaphoreType.DMA((2, 6, n)),
        ],
        compiler_params=pltpu.CompilerParams(
            collective_id=0, has_side_effects=True, vmem_limit_bytes=56 * 1024 * 1024
        ),
        name="level",
    )(
        neighbours, rotations, features, cotangent,
        w_first.reshape(9 * C, C), b_first.reshape(1, C), w_second.reshape(9 * C, C),
    )
    pooled, gin, gw1, gb1, gw2 = pl.pallas_call(
        functools.partial(finish, C),
        out_shape=(
            jax.ShapeDtypeStruct((H, H, C), BF16),
            jax.ShapeDtypeStruct((T, T, C), BF16),
            jax.ShapeDtypeStruct((3, 3, C, C), F32),
            jax.ShapeDtypeStruct((1, C), F32),
            jax.ShapeDtypeStruct((3, 3, C, C), F32),
        ),
        in_specs=[vm] * 3,
        out_specs=(vm,) * 5,
        compiler_params=pltpu.CompilerParams(vmem_limit_bytes=24 * 1024 * 1024),
        name="finish",
    )(pooled, gin, gath)
    return (pooled, gin, gw1, gb1.reshape(C), gw2)


def solution(mesh):
    tiles = P(("face", "sub"), None, None)
    return jax.shard_map(
        functools.partial(local, mesh.shape["sub"], mesh.shape["face"]),
        mesh=mesh,
        in_specs=(tiles, P(), P(), P(), P(), P(), tiles),
        out_specs=(tiles, tiles, P(), P(), P()),
        check_vma=False,
    )
```

profile of v0, /device:TPU:0, one launch (start us, length us, event | category | flops | bytes accessed | tf_op | source)
XLA Modules:
  0.0 72.9 jit_solution(9284528696558696674)
XLA Ops:
  0.6 1.4 %copy.12.nbr = s32[32,4]{1,0:T(8,128)} copy(s32[32,4]{0,1:T(4,128)} %param.11) | data formatting | bytes 1024 | tf_op args[4]
  2.0 1.4 %copy.13.rot = s32[32,4]{1,0:T(8,128)} copy(s32[32,4]{0,1:T(4,128)} %param.12) | data formatting | bytes 1024 | tf_op args[5]
  3.4 64.2 %level.1 = (bf16[12,12,192]{2,1,0:T(8,128)(2,1)}, bf16[24,24,192]{2,1,0:T(8,128)(2,1)}, bf16[2,3072,128]{2,1,0:T(8,128)(2,1)}) custom-call(s32[32,4]{1,0:T(8,128)} %copy.12.nbr, s32[32,4]{1,0:T(8,128)} %copy.13.rot, bf16[24,24,192]{2,1,0:T(8,128)(2,1)} %feat.1, bf16[12,12,192]{2,1,0:T(8,128)(2,1)} %cot.1, bf16[1728,192]{1,0:T(8,128)(2,1)} %bitcast.4, ...), custom_call_target="tpu_custom_call" | custom-call | tf_op jit(solution)/shard_map/level/pallas_call | solution.py:404
  67.6 0.0 copy-start
  67.6 1.4 %copy-done = bf16[2,3072,128]{2,1,0:T(8,128)(2,1)S(1)} copy-done((bf16[2,3072,128]{2,1,0:T(8,128)(2,1)S(1)}, bf16[2,3072,128]{2,1,0:T(8,128)(2,1)}, u32[]{:S(2)}) %copy-start) | copy-done | bytes 1572888
  69.0 0.0 copy-start.1
  69.0 1.0 %copy-done.1 = bf16[24,24,192]{2,1,0:T(8,128)(2,1)S(1)} copy-done((bf16[24,24,192]{2,1,0:T(8,128)(2,1)S(1)}, bf16[24,24,192]{2,1,0:T(8,128)(2,1)}, u32[]{:S(2)}) %copy-start.1) | copy-done | bytes 221208
  70.0 0.0 copy-start.2
  70.0 0.9 %copy-done.2 = bf16[12,12,192]{2,1,0:T(8,128)(2,1)S(1)} copy-done((bf16[12,12,192]{2,1,0:T(8,128)(2,1)S(1)}, bf16[12,12,192]{2,1,0:T(8,128)(2,1)}, u32[]{:S(2)}) %copy-start.2) | copy-done | bytes 55320
  70.9 2.0 %finish.1 = (bf16[12,12,192]{2,1,0:T(8,128)(2,1)}, bf16[24,24,192]{2,1,0:T(8,128)(2,1)}, f32[3,3,192,192]{3,2,1,0:T(8,128)}, f32[1,192]{1,0:T(1,128)}, f32[3,3,192,192]{3,2,1,0:T(8,128)}) custom-call(bf16[12,12,192]{2,1,0:T(8,128)(2,1)S(1)} %copy-done.2, bf16[24,24,192]{2,1,0:T(8,128)(2,1)S(1)} %copy-done.1, bf16[2,3072,128]{2,1,0:T(8,128)(2,1)S(1)} %copy-done), custom_call_target="tpu_custom_call" | custom-call | tf_op jit(solution)/shard_map/finish/pallas_call | solution.py:453
Async XLA Ops:
  67.6 1.4 %copy-start = (bf16[2,3072,128]{2,1,0:T(8,128)(2,1)S(1)}, bf16[2,3072,128]{2,1,0:T(8,128)(2,1)}, u32[]{:S(2)}) copy-start(bf16[2,3072,128]{2,1,0:T(8,128)(2,1)} %get-tuple-element.15.gath) | copy-start | bytes 4718596
  69.0 1.0 %copy-start.1 = (bf16[24,24,192]{2,1,0:T(8,128)(2,1)S(1)}, bf16[24,24,192]{2,1,0:T(8,128)(2,1)}, u32[]{:S(2)}) copy-start(bf16[24,24,192]{2,1,0:T(8,128)(2,1)} %get-tuple-element.14.gin_in) | copy-start | bytes 663556
  70.0 0.9 %copy-start.2 = (bf16[12,12,192]{2,1,0:T(8,128)(2,1)S(1)}, bf16[12,12,192]{2,1,0:T(8,128)(2,1)}, u32[]{:S(2)}) copy-start(bf16[12,12,192]{2,1,0:T(8,128)(2,1)} %get-tuple-element.13.pooled_in) | copy-start | bytes 165892
where the time goes:
time: 74 us; the launch traced here: 72.9 us
  Pallas kernels  66.3 us (90%)
  local copies, waits for them, and re-layouts  5.99 us (8%)
    pallas_call x1, Pallas kernels, local(): pl.pallas_call(functools.partial(kernel, S, F, chunk, scale), out_shape=(...  64.2 us
    unnamed x8, local copies, waits for them, and re-layouts  5.99 us
    pallas_call x1, Pallas kernels, local(): pl.pallas_call(functools.partial(finish, C), out_shape=(jax.ShapeDtypeStr...  2.04 us

commit v1 on v0

--- a/solution.py
+++ b/solution.py
@@ -79,12 +79,12 @@
         recv_mat[pl.ds(base, W), :] = hot((c32 == edge * W + p32) & (p32 < T) & (edge >= 0))
 
     def edge_code(tile, e):
-        r = rot[tile, e]
+        r = rot[e, tile]
         x = (e + 2) % 4
         src = (x + r) & 3
         odd = x % 2
         flip = jnp.where(r == 2, 1, jnp.where(r == 1, odd, jnp.where(r == 3, 1 - odd, 0)))
-        return nbr[tile, e] == me, src, flip
+        return nbr[e, tile] == me, src, flip
 
     def in_face(j, c):
         hit, src, flip, edge = jnp.int32(0), jnp.int32(0), jnp.int32(0), jnp.int32(-1)
@@ -93,7 +93,7 @@
             hit = jnp.where(h, 1, hit)
             src = jnp.where(h, s, src)
             flip = jnp.where(h, f, flip)
-            edge = jnp.where(nbr[me, e] == face * S + j, e, edge)
+            edge = jnp.where(nbr[e, me] == face * S + j, e, edge)
         put_slot(j, hit, src, flip, edge)
         return c
 
@@ -104,7 +104,7 @@
             h, s, fl = edge_code(f * S + sub, e)
             other = f != face
             hit = jnp.where(h & other, 1, 0)
-            edge = jnp.where((nbr[me, e] == f * S + sub) & other, e, -1)
+            edge = jnp.where((nbr[e, me] == f * S + sub) & other, e, -1)
             put_slot(S + f * 4 + e, hit, s, fl, edge)
         return c
 
@@ -114,33 +114,36 @@
         ex_in[ph, pl.ds(pl.multiple_of(sub * W, W), W), :] = jnp.zeros((W, C), BF16)
         ex_in[ph, pl.ds(pl.multiple_of((S + 4 * face) * W, W), 4 * W), :] = jnp.zeros((4 * W, C), BF16)
 
-    def ex_sub(ph, j, s_in, r_idx):
+    def ex_sub(ph, j, s_in):
         return pltpu.make_async_remote_copy(
             src_ref=ex_out.at[ph, pl.ds(pl.multiple_of(j * W, W), W), :],
             dst_ref=ex_in.at[ph, pl.ds(pl.multiple_of(s_in * W, W), W), :],
-            send_sem=ex_ss.at[ph, j], recv_sem=ex_rs.at[ph, r_idx],
+            send_sem=ex_ss.at[ph], recv_sem=ex_rs.at[ph],
             device_id=(face, j), device_id_type=MESH)
 
     def ex_face(ph, f, f_in):
         return pltpu.make_async_remote_copy(
             src_ref=ex_out.at[ph, pl.ds(pl.multiple_of((S + 4 * f) * W, W), 4 * W), :],
             dst_ref=ex_in.at[ph, pl.ds(pl.multiple_of((S + 4 * f_in) * W, W), 4 * W), :],
-            send_sem=ex_ss.at[ph, S + f], recv_sem=ex_rs.at[ph, S + f_in],
+            send_sem=ex_ss.at[ph], recv_sem=ex_rs.at[ph],
             device_id=(f, sub), device_id_type=MESH)
 
     def ex_start(ph, mat, rims):
         ex_out[ph] = dot(mat[...], rims).astype(BF16)
-        peers(S, sub, lambda j: ex_sub(ph, j, sub, sub).start())
+        peers(S, sub, lambda j: ex_sub(ph, j, sub).start())
         peers(F, face, lambda f: ex_face(ph, f, face).start())
 
+    def take(ref, sem):
+        pltpu.make_async_copy(ref, ref, sem).wait()
+
+    ex_rows = (S - 1) * W + (F - 1) * 4 * W
+
     def ex_wait(ph, mat):
-        peers(S, sub, lambda j: ex_sub(ph, j, j, j).wait_recv())
-        peers(F, face, lambda f: ex_face(ph, f, f).wait_recv())
+        take(ex_in.at[ph, 0:ex_rows, :], ex_rs.at[ph])
         return dot(mat[...], ex_in[ph], 0, 0)
 
     def ex_drain(ph):
-        peers(S, sub, lambda j: ex_sub(ph, j, sub, sub).wait_send())
-        peers(F, face, lambda f: ex_face(ph, f, face).wait_send())
+        take(ex_out.at[ph, 0:ex_rows, :], ex_ss.at[ph])
 
     own_rims = hot(iota((4 * W, M), 1) == rim_pos(iota((4 * W, 1), 0), T, 0))
     pad_rims = hot(iota((4 * W, MP), 1) == rim_pos(iota((4 * W, 1), 0), T, 1))
@@ -233,25 +236,25 @@
 
     rows = wf.shape[1]
 
-    def face_copy(k, st, f, f_in):
+    def face_copy(k, f, f_in):
         return pltpu.make_async_remote_copy(
             src_ref=wb.at[k, pl.ds(pl.multiple_of(f * part, 16), part), :],
             dst_ref=w1in.at[k, f_in],
-            send_sem=w_ss.at[k, 0, f], recv_sem=w_rs.at[k, 0, f_in],
+            send_sem=w_ss.at[k, 0], recv_sem=w_rs.at[k, 0],
             device_id=(f, sub), device_id_type=MESH)
 
     def b_copy(k, j, j_in):
         return pltpu.make_async_remote_copy(
             src_ref=red.at[k, pl.ds(pl.multiple_of(j * group, 16), group), :],
             dst_ref=w2in.at[k, j_in],
-            send_sem=w_ss.at[k, 1, j], recv_sem=w_rs.at[k, 1, j_in],
+            send_sem=w_ss.at[k, 1], recv_sem=w_rs.at[k, 1],
             device_id=(face, a_id * B + j), device_id_type=MESH)
 
     def a_copy(k, j, j_in):
         return pltpu.make_async_remote_copy(
             src_ref=red2.at[k, pl.ds(pl.multiple_of(j * chunk, 16), chunk), :],
             dst_ref=w3in.at[k, j_in],
-            send_sem=w_ss.at[k, 2, j], recv_sem=w_rs.at[k, 2, j_in],
+            send_sem=w_ss.at[k, 2], recv_sem=w_rs.at[k, 2],
             device_id=(face, j * B + b_id), device_id_type=MESH)
 
     def spot(k, start, size):
@@ -261,25 +264,34 @@
         place = spot(k, face * part + b_id * group + own * chunk, chunk)
         return pltpu.make_async_remote_copy(
             src_ref=place, dst_ref=place,
-            send_sem=w_ss.at[k, 3, j], recv_sem=w_rs.at[k, 3, own],
+            send_sem=w_ss.at[k, 3], recv_sem=w_rs.at[k, 3],
             device_id=(face, j * B + b_id), device_id_type=MESH)
 
     def b_gather(k, j, own):
         place = spot(k, face * part + own * group, group)
         return pltpu.make_async_remote_copy(
             src_ref=place, dst_ref=place,
-            send_sem=w_ss.at[k, 4, j], recv_sem=w_rs.at[k, 4, own],
+            send_sem=w_ss.at[k, 4], recv_sem=w_rs.at[k, 4],
             device_id=(face, a_id * B + j), device_id_type=MESH)
 
     def face_gather(k, f, own):
         place = spot(k, own * part, part)
         return pltpu.make_async_remote_copy(
             src_ref=place, dst_ref=place,
-            send_sem=w_ss.at[k, 5, f], recv_sem=w_rs.at[k, 5, own],
+            send_sem=w_ss.at[k, 5], recv_sem=w_rs.at[k, 5],
             device_id=(f, sub), device_id_type=MESH)
 
+    sizes = ((F - 1) * part, (B - 1) * group, (A - 1) * chunk, (A - 1) * chunk, (B - 1) * group, (F - 1) * part)
+
+    counts = (F - 1, B - 1, A - 1)
+
+    def arrived_all(k, st):
+        if sizes[st]:
+            slots = (w1in, w2in, w3in)
+            take(slots[st].at[k, 0:counts[st]] if st < 3 else gath.at[k, 0:sizes[st], :], w_rs.at[k, st])
+
     def reduce_start(k):
-        peers(F, face, lambda f: face_copy(k, 0, f, face).start())
+        peers(F, face, lambda f: face_copy(k, f, face).start())
 
     def summed(first, count, mine, ref, k):
         def step(d, tot):
@@ -287,7 +299,7 @@
         return lax.fori_loop(1, count, step, first)
 
     def reduce_b(k):
-        peers(F, face, lambda f: face_copy(k, 0, f, f).wait_recv())
+        arrived_all(k, 0)
         for r in range(B):
             at = pl.ds(pl.multiple_of(face * part + r * group, 16), group)
             tot = wf[k, at, :]
@@ -298,37 +310,34 @@
         peers(B, b_id, lambda j: b_copy(k, j, b_id).start())
 
     def reduce_a(k):
-        peers(B, b_id, lambda j: b_copy(k, j, j).wait_recv())
+        arrived_all(k, 1)
         tot = summed(accf[k, pl.ds(pl.multiple_of(b_id * group, 16), group), :], B, b_id, w2in, k)
         acc2[k] = tot
         red2[k] = tot.astype(BF16)
         peers(A, a_id, lambda j: a_copy(k, j, a_id).start())
 
     def gather_a(k):
-        peers(A, a_id, lambda j: a_copy(k, j, j).wait_recv())
+        arrived_all(k, 2)
         tot = summed(acc2[k, pl.ds(pl.multiple_of(a_id * chunk, 16), chunk), :], A, a_id, w3in, k)
         own = pl.ds(pl.multiple_of(face * part + b_id * group + a_id * chunk, 16), chunk)
         gath[k, own, :] = (tot * scale).astype(BF16)
         peers(A, a_id, lambda j: a_gather(k, j, a_id).start())
 
     def gather_b(k):
-        peers(A, a_id, lambda j: a_gather(k, j, j).wait_recv())
+        arrived_all(k, 3)
         peers(B, b_id, lambda j: b_gather(k, j, b_id).start())
 
     def gather_face(k):
-        peers(B, b_id, lambda j: b_gather(k, j, j).wait_recv())
+        arrived_all(k, 4)
         peers(F, face, lambda f: face_gather(k, f, face).start())
 
     def gather_end(k):
-        peers(F, face, lambda f: face_gather(k, f, f).wait_recv())
+        arrived_all(k, 5)
 
     def drain(k):
-        peers(F, face, lambda f: face_copy(k, 0, f, face).wait_send())
-        peers(B, b_id, lambda j: b_copy(k, j, b_id).wait_send())
-        peers(A, a_id, lambda j: a_copy(k, j, a_id).wait_send())
-        peers(A, a_id, lambda j: a_gather(k, j, a_id).wait_send())
-        peers(B, b_id, lambda j: b_gather(k, j, b_id).wait_send())
-        peers(F, face, lambda f: face_gather(k, f, face).wait_send())
+        for st in range(6):
+            if sizes[st]:
+                take((wb, red, red2, gath, gath, gath)[st].at[k, 0:sizes[st], :], w_ss.at[k, st])
 
     for k in range(2):
         put(k, 14 * C, jnp.zeros((rows - 14 * C, LANES), F32))
@@ -400,13 +409,12 @@
     scale = 1.0 / math.sqrt(D * T * T)
     vm = pl.BlockSpec(memory_space=pltpu.VMEM)
     sm = pl.BlockSpec(memory_space=pltpu.SMEM)
-    n = max(S, F)
     pooled, gin, gath = pl.pallas_call(
         functools.partial(kernel, S, F, chunk, scale),
         out_shape=(
-            jax.ShapeDtypeStruct((H, H, C), BF16),
-            jax.ShapeDtypeStruct((T, T, C), BF16),
-            jax.ShapeDtypeStruct((2, rows, LANES), BF16),
+            pltpu.VMEM((H, H, C), BF16),
+            pltpu.VMEM((T, T, C), BF16),
+            pltpu.VMEM((2, rows, LANES), BF16),
         ),
         in_specs=[sm, sm, vm, vm, vm, vm, vm],
         out_specs=(vm,) * 3,
@@ -437,17 +445,17 @@
             pltpu.VMEM((2, A * chunk, LANES), BF16),
             pltpu.VMEM((2, A * chunk, LANES), F32),
             pltpu.VMEM((2, A, chunk, LANES), BF16),
-            pltpu.SemaphoreType.DMA((4, S + F)),
-            pltpu.SemaphoreType.DMA((4, S + F)),
-            pltpu.SemaphoreType.DMA((2, 6, n)),
-            pltpu.SemaphoreType.DMA((2, 6, n)),
+            pltpu.SemaphoreType.DMA((4,)),
+            pltpu.SemaphoreType.DMA((4,)),
+            pltpu.SemaphoreType.DMA((2, 6)),
+            pltpu.SemaphoreType.DMA((2, 6)),
         ],
         compiler_params=pltpu.CompilerParams(
             collective_id=0, has_side_effects=True, vmem_limit_bytes=56 * 1024 * 1024
         ),
         name="level",
     )(
-        neighbours, rotations, features, cotangent,
+        neighbours.T, rotations.T, features, cotangent,
         w_first.reshape(9 * C, C), b_first.reshape(1, C), w_second.reshape(9 * C, C),
     )
     pooled, gin, gw1, gb1, gw2 = pl.pallas_call(

time: 74 us -> 61.6 us (0.83); the launches traced: 72.9 us -> 61.4 us
  local copies, waits for them, and re-layouts: 5.99 us -> 0 us
  Pallas kernels: 66.3 us -> 60.8 us
    unnamed x8 -> x0, local copies, waits for them, and re-layouts: 5.99 us -> none
    pallas_call x1, Pallas kernels: 64.2 us -> 58.7 us  [local(): pl.pallas_call(functools.partial(kernel, S, F, chunk, scale), out_shape=(...]
where the time goes in v1:
time: 61.6 us; the launch traced here: 61.4 us
  Pallas kernels  60.8 us (99%)
  between operations  0.64 us (1%)
    pallas_call x1, Pallas kernels, local(): pl.pallas_call(functools.partial(kernel, S, F, chunk, scale), out_shape=(...  58.7 us
    pallas_call x1, Pallas kernels, local(): pl.pallas_call(functools.partial(finish, C), out_shape=(jax.ShapeDtypeStr...  2.04 us

profile of v1, /device:TPU:0, one launch (start us, length us, event | category | flops | bytes accessed | tf_op | source)
XLA Modules:
  0.0 61.4 jit_solution(13107047213050307729)
XLA Ops:
  0.6 58.7 %level.1 = (bf16[12,12,192]{2,1,0:T(8,128)(2,1)S(1)}, bf16[24,24,192]{2,1,0:T(8,128)(2,1)S(1)}, bf16[2,3072,128]{2,1,0:T(8,128)(2,1)S(1)}) custom-call(s32[4,32]{1,0:T(4,128)} %bitcast.8, s32[4,32]{1,0:T(4,128)} %bitcast.9, bf16[24,24,192]{2,1,0:T(8,128)(2,1)} %feat.1, bf16[12,12,192]{2,1,0:T(8,128)(2,1)} %cot.1, bf16[1728,192]{1,0:T(8,128)(2,1)} %bitcast.6, ...), custom_call_target="tpu_custom_call" | custom-call | tf_op jit(solution)/shard_map/level/pallas_call | solution.py:412
  59.4 2.0 %finish.1 = (bf16[12,12,192]{2,1,0:T(8,128)(2,1)}, bf16[24,24,192]{2,1,0:T(8,128)(2,1)}, f32[3,3,192,192]{3,2,1,0:T(8,128)}, f32[1,192]{1,0:T(1,128)}, f32[3,3,192,192]{3,2,1,0:T(8,128)}) custom-call(bf16[12,12,192]{2,1,0:T(8,128)(2,1)S(1)} %get-tuple-element.13.pooled_in, bf16[24,24,192]{2,1,0:T(8,128)(2,1)S(1)} %get-tuple-element.14.gin_in, ...), custom_call_target="tpu_custom_call" | custom-call | tf_op jit(solution)/shard_map/finish/pallas_call | solution.py:461

commit v2 on v1

--- a/solution.py
+++ b/solution.py
@@ -10,6 +10,7 @@
 
 LANES = 128
 W = 32
+LOW = 16
 F32, BF16 = jnp.float32, jnp.bfloat16
 MESH = pl.DeviceIdType.MESH
 
@@ -42,12 +43,13 @@
     return ((r >> 6) << 4) + ((r & (W - 1)) >> 1)
 
 
-def kernel(S, F, chunk, scale, nbr, rot, feat, cot, w1, b1, w2,
+def kernel(S, F, chunk, scale, nbr_hbm, rot_hbm, feat_hbm, cot_hbm, w1_hbm, b1_hbm, w2_hbm,
            pooled, gin, gath,
-           send_mat, recv_mat, pad_in, pad_act, gpad1, gpad2, cotp,
+           nbr, rot, feat, cot, w1, b1, w2,
+           send_mat, recv_mat, send_low, recv_low, pad_in, pad_act, gpad1, gpad2, cotp,
            win_in, win_act, gs1, gs2, hidden, second, pg, gact,
            ex_out, ex_in, wf, wb, w1in, red, accf, w2in, red2, acc2, w3in,
-           ex_ss, ex_rs, w_ss, w_rs):
+           ex_ss, ex_rs, w_ss, w_rs, in_sem):
     T, C = feat.shape[0], feat.shape[2]
     H = T // 2
     face, sub = lax.axis_index("face"), lax.axis_index("sub")
@@ -69,14 +71,31 @@
     peers(S, sub, lambda j: pl.semaphore_signal(barrier, inc=1, device_id=(face, j), device_id_type=MESH))
     peers(F, face, lambda f: pl.semaphore_signal(barrier, inc=1, device_id=(f, sub), device_id_type=MESH))
 
+    def load(i):
+        pairs = ((nbr_hbm, nbr), (rot_hbm, rot), (feat_hbm, feat), (w2_hbm, w2), (cot_hbm, cot), (w1_hbm, w1), (b1_hbm, b1))
+        return pltpu.make_async_copy(pairs[i][0], pairs[i][1], in_sem.at[i])
+
+    for i in (2, 0, 1, 3, 4, 5, 6):
+        load(i).start()
+
     p32 = iota((W, 4 * W), 0)
     c32 = iota((W, 4 * W), 1)
 
-    def put_slot(k, hit, src, flip, edge):
+    q16 = iota((LOW, 8 * W), 0)
+    d16 = iota((LOW, 8 * W), 1)
+    low_pix = q16 + jnp.where(d16 >= 4 * W, H, 0)
+    low_col = d16 & (4 * W - 1)
+
+    def put_send(k, hit, src, flip):
         tgt = jnp.where(flip == 1, src * W + T - 1 - p32, src * W + p32)
-        base = pl.multiple_of(k * W, W)
-        send_mat[pl.ds(base, W), :] = hot((c32 == tgt) & (p32 < T) & (hit == 1))
-        recv_mat[pl.ds(base, W), :] = hot((c32 == edge * W + p32) & (p32 < T) & (edge >= 0))
+        send_mat[pl.ds(pl.multiple_of(k * W, W), W), :] = hot((c32 == tgt) & (p32 < T) & (hit == 1))
+        tgt = jnp.where(flip == 1, src * W + T - 1 - low_pix, src * W + low_pix)
+        send_low[pl.ds(pl.multiple_of(k * LOW, LOW), LOW), :] = hot((low_col == tgt) & (q16 < H) & (hit == 1))
+
+    def put_recv(k, edge):
+        recv_mat[pl.ds(pl.multiple_of(k * W, W), W), :] = hot((c32 == edge * W + p32) & (p32 < T) & (edge >= 0))
+        recv_low[pl.ds(pl.multiple_of(k * LOW, LOW), LOW), :] = hot(
+            (low_col == edge * W + low_pix) & (q16 < H) & (edge >= 0))
 
     def edge_code(tile, e):
         r = rot[e, tile]
@@ -86,94 +105,94 @@
         flip = jnp.where(r == 2, 1, jnp.where(r == 1, odd, jnp.where(r == 3, 1 - odd, 0)))
         return nbr[e, tile] == me, src, flip
 
-    def in_face(j, c):
-        hit, src, flip, edge = jnp.int32(0), jnp.int32(0), jnp.int32(0), jnp.int32(-1)
+    def send_in_face(j, c):
+        hit, src, flip = jnp.int32(0), jnp.int32(0), jnp.int32(0)
         for e in range(4):
             h, s, f = edge_code(face * S + j, e)
             hit = jnp.where(h, 1, hit)
             src = jnp.where(h, s, src)
             flip = jnp.where(h, f, flip)
-            edge = jnp.where(nbr[e, me] == face * S + j, e, edge)
-        put_slot(j, hit, src, flip, edge)
+        put_send(j, hit, src, flip)
         return c
 
-    lax.fori_loop(0, S, in_face, 0)
-
-    def cross(f, c):
+    def send_cross(f, c):
         for e in range(4):
             h, s, fl = edge_code(f * S + sub, e)
-            other = f != face
-            hit = jnp.where(h & other, 1, 0)
-            edge = jnp.where((nbr[e, me] == f * S + sub) & other, e, -1)
-            put_slot(S + f * 4 + e, hit, s, fl, edge)
+            put_send(S + f * 4 + e, jnp.where(h & (f != face), 1, 0), s, fl)
         return c
 
-    lax.fori_loop(0, F, cross, 0)
-
-    for ph in range(4):
-        ex_in[ph, pl.ds(pl.multiple_of(sub * W, W), W), :] = jnp.zeros((W, C), BF16)
-        ex_in[ph, pl.ds(pl.multiple_of((S + 4 * face) * W, W), 4 * W), :] = jnp.zeros((4 * W, C), BF16)
+    def recv_in_face(j, c):
+        edge = jnp.int32(-1)
+        for e in range(4):
+            edge = jnp.where(nbr[e, me] == face * S + j, e, edge)
+        put_recv(j, edge)
+        return c
+
+    def recv_cross(f, c):
+        for e in range(4):
+            put_recv(S + f * 4 + e, jnp.where((nbr[e, me] == f * S + sub) & (f != face), e, -1))
+        return c
 
     def ex_sub(ph, j, s_in):
         return pltpu.make_async_remote_copy(
-            src_ref=ex_out.at[ph, pl.ds(pl.multiple_of(j * W, W), W), :],
-            dst_ref=ex_in.at[ph, pl.ds(pl.multiple_of(s_in * W, W), W), :],
+            src_ref=ex_out.at[ph, j], dst_ref=ex_in.at[ph, s_in],
             send_sem=ex_ss.at[ph], recv_sem=ex_rs.at[ph],
             device_id=(face, j), device_id_type=MESH)
 
     def ex_face(ph, f, f_in):
         return pltpu.make_async_remote_copy(
-            src_ref=ex_out.at[ph, pl.ds(pl.multiple_of((S + 4 * f) * W, W), 4 * W), :],
-            dst_ref=ex_in.at[ph, pl.ds(pl.multiple_of((S + 4 * f_in) * W, W), 4 * W), :],
+            src_ref=ex_out.at[ph, pl.ds(S + 4 * f, 4)], dst_ref=ex_in.at[ph, pl.ds(S + 4 * f_in, 4)],
             send_sem=ex_ss.at[ph], recv_sem=ex_rs.at[ph],
             device_id=(f, sub), device_id_type=MESH)
 
-    def ex_start(ph, mat, rims):
-        ex_out[ph] = dot(mat[...], rims).astype(BF16)
+    slots = S + 4 * F
+    R = C - LANES
+
+    def ex_start(ph, mat, low, rims):
+        zero = jnp.zeros((4 * W, R), BF16)
+        wide = jnp.concatenate([
+            jnp.concatenate([rims[:, LANES:C], zero], axis=1),
+            jnp.concatenate([zero, rims[:, LANES:C]], axis=1)], axis=0)
+        ex_out[ph, :, 0:W, :] = dot(mat[...], rims[:, 0:LANES]).astype(BF16).reshape(slots, W, LANES)
+        ex_out[ph, :, W:W + LOW, :] = dot(low[...], wide).astype(BF16).reshape(slots, LOW, LANES)
+        peers(F, face, lambda f: ex_face(ph, f, face).start())
         peers(S, sub, lambda j: ex_sub(ph, j, sub).start())
-        peers(F, face, lambda f: ex_face(ph, f, face).start())
 
     def take(ref, sem):
         pltpu.make_async_copy(ref, ref, sem).wait()
 
-    ex_rows = (S - 1) * W + (F - 1) * 4 * W
-
-    def ex_wait(ph, mat):
-        take(ex_in.at[ph, 0:ex_rows, :], ex_rs.at[ph])
-        return dot(mat[...], ex_in[ph], 0, 0)
+    ex_count = S - 1 + (F - 1) * 4
+
+    def ex_wait(ph, mat, low):
+        take(ex_in.at[ph, 0:ex_count], ex_rs.at[ph])
+        left = dot(mat[...], ex_in[ph, :, 0:W, :].reshape(slots * W, LANES), 0, 0)
+        rest = dot(low[...], ex_in[ph, :, W:W + LOW, :].reshape(slots * LOW, LANES), 0, 0)
+        rest = rest[0:4 * W, 0:R] + rest[4 * W:8 * W, R:2 * R]
+        return jnp.concatenate([left, rest], axis=1)
 
     def ex_drain(ph):
-        take(ex_out.at[ph, 0:ex_rows, :], ex_ss.at[ph])
+        take(ex_out.at[ph, 0:ex_count], ex_ss.at[ph])
 
     own_rims = hot(iota((4 * W, M), 1) == rim_pos(iota((4 * W, 1), 0), T, 0))
-    pad_rims = hot(iota((4 * W, MP), 1) == rim_pos(iota((4 * W, 1), 0), T, 1))
-    own_place = hot(iota((M, 4 * W), 0) == rim_pos(iota((1, 4 * W), 1), T, 0))
-    pad_place = hot(iota((MP, 4 * W), 0) == rim_pos(iota((1, 4 * W), 1), T, 1))
 
     def windows(src, dst, rows):
         for b in range(3):
             dst[b] = src[:, b:b + W, :].reshape(rows * W, C).astype(BF16)
 
     def add_halo(padded, halo):
+        pad_place = hot(iota((MP, 4 * W), 0) == rim_pos(iota((1, 4 * W), 1), T, 1))
         placed = dot(pad_place, halo.astype(BF16)).reshape(T + 2, W, C)
         padded[:, 0:W, :] = padded[:, 0:W, :] + placed
 
-    def conv(win, wt, out, rows, back):
-        half = rows
-
-        def step(i, c):
-            acc = None
-            for a in range(3):
-                for b in range(3):
-                    off = pl.multiple_of(i * half, 16) + a * W
-                    x = win[b, pl.ds(pl.multiple_of(off, 16), half), :]
-                    tap = (2 - a) * 3 + 2 - b if back else a * 3 + b
-                    d = dot(x, wt[tap * C:(tap + 1) * C, :], 1, 1 if back else 0)
-                    acc = d if acc is None else acc + d
-            out[pl.ds(pl.multiple_of(i * half, 16), half), :] = acc
-            return c
-
-        lax.fori_loop(0, 1, step, 0)
+    def conv(win, wt, out, lo, n, back):
+        acc = None
+        for a in range(3):
+            for b in range(3):
+                x = win[b, lo + a * W:lo + a * W + n, :]
+                tap = (2 - a) * 3 + 2 - b if back else a * 3 + b
+                d = dot(x, wt[tap * C:(tap + 1) * C, :], 1, 1 if back else 0)
+                acc = d if acc is None else acc + d
+        out[lo:lo + n, :] = acc
 
     def put(k, r, v):
         wf[k, r:r + v.shape[0], :] = v
@@ -193,43 +212,61 @@
                 put(k, (9 + t // 2) * C, pair)
 
     pad_in[...] = jnp.zeros(pad_in.shape, F32)
+    load(2).wait()
     pad_in[1:T + 1, 1:T + 1, :] = feat[...].astype(F32)
     flat_in = pad_in[1:T + 1, 1:W + 1, :].reshape(M, C)
     rims = dot(own_rims, flat_in.astype(BF16)).astype(BF16)
+    load(0).wait()
+    load(1).wait()
+    lax.fori_loop(0, S, send_in_face, 0)
+    lax.fori_loop(0, F, send_cross, 0)
     pl.semaphore_wait(barrier, S + F - 2)
-    ex_start(0, send_mat, rims)
-
+    ex_start(0, send_mat, send_low, rims)
+
+    lax.fori_loop(0, S, recv_in_face, 0)
+    lax.fori_loop(0, F, recv_cross, 0)
     cotp[...] = jnp.zeros(cotp.shape, F32)
+    load(4).wait()
     cotp[:, 0:H, :] = cot[...].astype(F32)
     spread = hot(pool_pos(iota((M, 1), 0)) == iota((M, H * 16), 1))
     up = dot(spread, cotp[...].reshape(H * 16, C).astype(BF16)) * 0.25
     gpad2[...] = jnp.zeros(gpad2.shape, F32)
     gpad2[2:T + 2, 2:T + 2, :] = up.reshape(T, W, C)[:, 0:T, :]
     windows(gpad2, gs2, T + 4)
-    conv(gs2, w2, pg, MP, True)
+    load(3).wait()
+    conv(gs2, w2, pg, 0, MP, True)
+    pad_rims = hot(iota((4 * W, MP), 1) == rim_pos(iota((4 * W, 1), 0), T, 1))
     rims = dot(pad_rims, pg[...].astype(BF16)).astype(BF16)
-    ex_start(2, recv_mat, rims)
+    ex_start(2, recv_mat, recv_low, rims)
     gact[...] = pg[...].reshape(T + 2, W, C)[1:T + 1]
     pad_act[...] = jnp.zeros(pad_act.shape, F32)
     gpad1[...] = jnp.zeros(gpad1.shape, F32)
-
-    add_halo(pad_in, ex_wait(0, recv_mat))
+    for ph in range(4):
+        ex_in[ph, sub] = jnp.zeros((W + LOW, LANES), BF16)
+        ex_in[ph, pl.ds(S + 4 * face, 4)] = jnp.zeros((4, W + LOW, LANES), BF16)
+
+    halo0 = ex_wait(0, recv_mat, recv_low)
+    add_halo(pad_in, halo0)
     windows(pad_in, win_in, T + 2)
-    conv(win_in, w1, hidden, M, False)
+    load(5).wait()
+    load(6).wait()
+    conv(win_in, w1, hidden, 0, M, False)
     hid = hidden[...] + b1[...]
     sig = 1.0 / (1.0 + jnp.exp(-hid))
     act = (hid * sig).astype(BF16)
     rims = dot(own_rims, act).astype(BF16)
-    ex_start(1, send_mat, rims)
+    ex_start(1, send_mat, send_low, rims)
     pad_act[1:T + 1, 1:T + 1, :] = act.astype(F32).reshape(T, W, C)[:, 0:T, :]
+    slope = (sig * (1.0 + hid * (1.0 - sig))).reshape(T, W, C)[:, 0:T, :]
 
     def fold(middle, arrived):
+        own_place = hot(iota((M, 4 * W), 0) == rim_pos(iota((1, 4 * W), 1), T, 0))
         hi, lo = split(arrived)
         back = dot(own_place, hi) + dot(own_place, lo)
         return middle[:, 1:T + 1, :] + back.reshape(T, W, C)[:, 0:T, :]
 
-    ga = fold(gact, ex_wait(2, send_mat)).astype(BF16).astype(F32)
-    slope = (sig * (1.0 + hid * (1.0 - sig))).reshape(T, W, C)[:, 0:T, :]
+    halo2 = ex_wait(2, send_mat, send_low)
+    ga = fold(gact, halo2).astype(BF16).astype(F32)
     gh = (ga * slope).astype(BF16).astype(F32)
     gpad1[2:T + 2, 2:T + 2, :] = gh
     windows(gpad1, gs1, T + 4)
@@ -348,32 +385,37 @@
     put(0, 14 * C, jnp.where(line == 0, bias[:, 0:LANES], jnp.where(line == 1, bias[:, LANES:], 0.0)))
     reduce_start(0)
 
-    add_halo(pad_act, ex_wait(1, recv_mat))
+    half = (T + 2) // 2 * W
+    conv(gs1, w1, pg, 0, half, True)
+    reduce_b(0)
+    conv(gs1, w1, pg, half, MP - half, True)
+    rims = dot(pad_rims, pg[...].astype(BF16)).astype(BF16)
+    ex_start(3, recv_mat, recv_low, rims)
+    halo1 = ex_wait(1, recv_mat, recv_low)
+    add_halo(pad_act, halo1)
     windows(pad_act, win_act, T + 2)
-    reduce_b(0)
     weight_grad(1, win_act, gs2)
     reduce_start(1)
-    conv(gs1, w1, pg, MP, True)
-    rims = dot(pad_rims, pg[...].astype(BF16)).astype(BF16)
-    ex_start(3, recv_mat, rims)
+    conv(win_act, w2, second, 0, M // 2, False)
+    reduce_b(1)
     reduce_a(0)
-    reduce_b(1)
-    conv(win_act, w2, second, M, False)
-    gather_a(0)
+    conv(win_act, w2, second, M // 2, M // 2, False)
     hi, lo = split(second[...] + pad_in[1:T + 1, 1:W + 1, :].reshape(M, C))
     mean = hot(pool_pos(iota((1, M), 1)) == iota((H * 16, M), 0))
     down = (dot(mean, hi) + dot(mean, lo)) * 0.25
     pooled[...] = down.reshape(H, 16, C)[:, 0:H, :].astype(BF16)
+    gather_a(0)
     reduce_a(1)
+    gact[...] = pg[...].reshape(T + 2, W, C)[1:T + 1]
+    halo3 = ex_wait(3, send_mat, send_low)
+    total = fold(gact, halo3) + gpad2[2:T + 2, 2:T + 2, :]
+    gin[...] = total.astype(BF16)
     gather_b(0)
-    gact[...] = pg[...].reshape(T + 2, W, C)[1:T + 1]
-    total = fold(gact, ex_wait(3, send_mat)) + gpad2[2:T + 2, 2:T + 2, :]
-    gin[...] = total.astype(BF16)
     gather_a(1)
+    gather_b(1)
     gather_face(0)
-    gather_b(1)
+    gather_face(1)
     gather_end(0)
-    gather_face(1)
     gather_end(1)
     for ph in range(4):
         ex_drain(ph)
@@ -405,10 +447,9 @@
     A = 4 if S % 4 == 0 else 1
     B = S // A
     rows, part = chunk * D, chunk * S
-    K = (S + 4 * F) * W
+    K = S + 4 * F
     scale = 1.0 / math.sqrt(D * T * T)
     vm = pl.BlockSpec(memory_space=pltpu.VMEM)
-    sm = pl.BlockSpec(memory_space=pltpu.SMEM)
     pooled, gin, gath = pl.pallas_call(
         functools.partial(kernel, S, F, chunk, scale),
         out_shape=(
@@ -416,11 +457,20 @@
             pltpu.VMEM((T, T, C), BF16),
             pltpu.VMEM((2, rows, LANES), BF16),
         ),
-        in_specs=[sm, sm, vm, vm, vm, vm, vm],
+        in_specs=[pl.BlockSpec(memory_space=pl.ANY)] * 7,
         out_specs=(vm,) * 3,
         scratch_shapes=[
-            pltpu.VMEM((K, 4 * W), BF16),
-            pltpu.VMEM((K, 4 * W), BF16),
+            pltpu.SMEM((4, D), jnp.int32),
+            pltpu.SMEM((4, D), jnp.int32),
+            pltpu.VMEM((T, T, C), BF16),
+            pltpu.VMEM((H, H, C), BF16),
+            pltpu.VMEM((9 * C, C), BF16),
+            pltpu.VMEM((1, C), F32),
+            pltpu.VMEM((9 * C, C), BF16),
+            pltpu.VMEM((K * W, 4 * W), BF16),
+            pltpu.VMEM((K * W, 4 * W), BF16),
+            pltpu.VMEM((K * LOW, 8 * W), BF16),
+            pltpu.VMEM((K * LOW, 8 * W), BF16),
             pltpu.VMEM((T + 2, W + 8, C), F32),
             pltpu.VMEM((T + 2, W + 8, C), F32),
             pltpu.VMEM((T + 4, W + 8, C), F32),
@@ -434,8 +484,8 @@
             pltpu.VMEM((T * W, C), F32),
             pltpu.VMEM(((T + 2) * W, C), F32),
             pltpu.VMEM((T, W, C), F32),
-            pltpu.VMEM((4, K, C), BF16),
-            pltpu.VMEM((4, K, C), BF16),
+            pltpu.VMEM((4, K, W + LOW, LANES), BF16),
+            pltpu.VMEM((4, K, W + LOW, LANES), BF16),
             pltpu.VMEM((2, rows, LANES), F32),
             pltpu.VMEM((2, rows, LANES), BF16),
             pltpu.VMEM((2, F, part, LANES), BF16),
@@ -449,6 +499,7 @@
             pltpu.SemaphoreType.DMA((4,)),
             pltpu.SemaphoreType.DMA((2, 6)),
             pltpu.SemaphoreType.DMA((2, 6)),
+            pltpu.SemaphoreType.DMA((7,)),
         ],
         compiler_params=pltpu.CompilerParams(
             collective_id=0, has_side_effects=True, vmem_limit_bytes=56 * 1024 * 1024

time: 61.6 us -> 54.1 us (0.88)
  Pallas kernels: 60.8 us -> 53.3 us
    pallas_call x1, Pallas kernels: 58.7 us -> 51.3 us  [local(): pl.pallas_call(functools.partial(kernel, S, F, chunk, scale), out_shape=(...]
where the time goes in v2:
time: 54.1 us; the launch traced here: 54 us
  Pallas kernels  53.3 us (99%)
  between operations  0.64 us (1%)
    pallas_call x1, Pallas kernels, local(): pl.pallas_call(functools.partial(kernel, S, F, chunk, scale), out_shape=(...  51.3 us
    pallas_call x1, Pallas kernels, local(): pl.pallas_call(functools.partial(finish, C), out_shape=(jax.ShapeDtypeStr...  2.04 us

profile of v2, /device:TPU:0, one launch (start us, length us, event | category | flops | bytes accessed | tf_op | source)
XLA Modules:
  0.0 54.0 jit_solution(10572652581078792615)
XLA Ops:
  0.6 51.3 %level.1 = (bf16[12,12,192]{2,1,0:T(8,128)(2,1)S(1)}, bf16[24,24,192]{2,1,0:T(8,128)(2,1)S(1)}, bf16[2,3072,128]{2,1,0:T(8,128)(2,1)S(1)}) custom-call(s32[4,32]{1,0:T(4,128)} %bitcast.8, s32[4,32]{1,0:T(4,128)} %bitcast.9, bf16[24,24,192]{2,1,0:T(8,128)(2,1)} %feat_hbm.1, bf16[12,12,192]{2,1,0:T(8,128)(2,1)} %cot_hbm.1, bf16[1728,192]{1,0:T(8,128)(2,1)} %bitcast.6, ...), custom_call_target="tpu_custom_call" | custom-call | tf_op jit(solution)/shard_map/level/pallas_call | solution.py:453
  51.9 2.0 %finish.1 = (bf16[12,12,192]{2,1,0:T(8,128)(2,1)}, bf16[24,24,192]{2,1,0:T(8,128)(2,1)}, f32[3,3,192,192]{3,2,1,0:T(8,128)}, f32[1,192]{1,0:T(1,128)}, f32[3,3,192,192]{3,2,1,0:T(8,128)}) custom-call(bf16[12,12,192]{2,1,0:T(8,128)(2,1)S(1)} %get-tuple-element.13.pooled_in, bf16[24,24,192]{2,1,0:T(8,128)(2,1)S(1)} %get-tuple-element.14.gin_in, ...), custom_call_target="tpu_custom_call" | custom-call | tf_op jit(solution)/shard_map/finish/pallas_call | solution.py:512

commit v3 on v2

--- a/solution.py
+++ b/solution.py
@@ -11,6 +11,7 @@
 LANES = 128
 W = 32
 LOW = 16
+PIECES = (5, 6)
 F32, BF16 = jnp.float32, jnp.bfloat16
 MESH = pl.DeviceIdType.MESH
 
@@ -43,7 +44,7 @@
     return ((r >> 6) << 4) + ((r & (W - 1)) >> 1)
 
 
-def kernel(S, F, chunk, scale, nbr_hbm, rot_hbm, feat_hbm, cot_hbm, w1_hbm, b1_hbm, w2_hbm,
+def kernel(S, F, pieces, scale, nbr_hbm, rot_hbm, feat_hbm, cot_hbm, w1_hbm, b1_hbm, w2_hbm,
            pooled, gin, gath,
            nbr, rot, feat, cot, w1, b1, w2,
            send_mat, recv_mat, send_low, recv_low, pad_in, pad_act, gpad1, gpad2, cotp,
@@ -54,11 +55,9 @@
     H = T // 2
     face, sub = lax.axis_index("face"), lax.axis_index("sub")
     me = face * S + sub
-    part = chunk * S
     A = 4 if S % 4 == 0 else 1
     B = S // A
     a_id, b_id = sub // B, lax.rem(sub, B)
-    group = chunk * A
     M, MP = T * W, (T + 2) * W
 
     def peers(count, mine, body):
@@ -153,8 +152,9 @@
         wide = jnp.concatenate([
             jnp.concatenate([rims[:, LANES:C], zero], axis=1),
             jnp.concatenate([zero, rims[:, LANES:C]], axis=1)], axis=0)
-        ex_out[ph, :, 0:W, :] = dot(mat[...], rims[:, 0:LANES]).astype(BF16).reshape(slots, W, LANES)
-        ex_out[ph, :, W:W + LOW, :] = dot(low[...], wide).astype(BF16).reshape(slots, LOW, LANES)
+        top = dot(mat[...], rims[:, 0:LANES]).reshape(slots, W, LANES)[:, 0:T, :]
+        bottom = dot(low[...], wide).reshape(slots, LOW, LANES)
+        ex_out[ph] = jnp.concatenate([top, bottom], axis=1).astype(BF16)
         peers(F, face, lambda f: ex_face(ph, f, face).start())
         peers(S, sub, lambda j: ex_sub(ph, j, sub).start())
 
@@ -165,8 +165,9 @@
 
     def ex_wait(ph, mat, low):
         take(ex_in.at[ph, 0:ex_count], ex_rs.at[ph])
-        left = dot(mat[...], ex_in[ph, :, 0:W, :].reshape(slots * W, LANES), 0, 0)
-        rest = dot(low[...], ex_in[ph, :, W:W + LOW, :].reshape(slots * LOW, LANES), 0, 0)
+        got = ex_in[ph].astype(F32)
+        left = dot(mat[...], got[:, 0:W, :].reshape(slots * W, LANES).astype(BF16), 0, 0)
+        rest = dot(low[...], got[:, T:T + LOW, :].reshape(slots * LOW, LANES).astype(BF16), 0, 0)
         rest = rest[0:4 * W, 0:R] + rest[4 * W:8 * W, R:2 * R]
         return jnp.concatenate([left, rest], axis=1)
 
@@ -194,22 +195,23 @@
                 acc = d if acc is None else acc + d
         out[lo:lo + n, :] = acc
 
-    def put(k, r, v):
-        wf[k, r:r + v.shape[0], :] = v
-        wb[k, r:r + v.shape[0], :] = v.astype(BF16)
-
-    def weight_grad(k, win, gs):
-        odd = None
+    def put(r, v):
+        wf[r:r + v.shape[0], :] = v
+        wb[r:r + v.shape[0], :] = v.astype(BF16)
+
+    def weight_grad(base, win, gs):
         for t in range(9):
             a, b = t // 3, t % 3
             v = dot(win[b], gs[2, (2 - a) * W:(2 - a) * W + MP, :], 0, 0)
-            put(k, t * C, v[:, 0:LANES])
+            at = base + t // 2 * 3 * C
+            put(at + t % 2 * C, v[:, 0:LANES])
             rest = v[:, LANES:C]
             if t % 2 == 0:
-                odd = rest
-            if t % 2 == 1 or t == 8:
-                pair = jnp.concatenate([odd, rest], axis=1)
-                put(k, (9 + t // 2) * C, pair)
+                even = rest
+            if t % 2 == 1:
+                put(at + 2 * C, jnp.concatenate([even, rest], axis=1))
+            if t == 8:
+                put(at + C, jnp.concatenate([rest, rest], axis=1))
 
     pad_in[...] = jnp.zeros(pad_in.shape, F32)
     load(2).wait()
@@ -242,8 +244,8 @@
     pad_act[...] = jnp.zeros(pad_act.shape, F32)
     gpad1[...] = jnp.zeros(gpad1.shape, F32)
     for ph in range(4):
-        ex_in[ph, sub] = jnp.zeros((W + LOW, LANES), BF16)
-        ex_in[ph, pl.ds(S + 4 * face, 4)] = jnp.zeros((4, W + LOW, LANES), BF16)
+        ex_in[ph, sub] = jnp.zeros((T + LOW, LANES), BF16)
+        ex_in[ph, pl.ds(S + 4 * face, 4)] = jnp.zeros((4, T + LOW, LANES), BF16)
 
     halo0 = ex_wait(0, recv_mat, recv_low)
     add_halo(pad_in, halo0)
@@ -271,170 +273,201 @@
     gpad1[2:T + 2, 2:T + 2, :] = gh
     windows(gpad1, gs1, T + 4)
 
-    rows = wf.shape[1]
-
-    def face_copy(k, f, f_in):
+    D = S * F
+    starts = [sum(pieces[:p]) for p in range(len(pieces))]
+
+    def whole(p, level):
+        share = (D // F, D // (F * B), 1)[level]
+        lo = starts[p] // D * share
+        return slice(lo, lo + pieces[p] // D * share)
+
+    def spot(ref, p, start, size):
+        return ref.at[pl.ds(pl.multiple_of(starts[p] + start, 16), size), :]
+
+    def sizes(p):
+        chunk = pieces[p] // D
+        return chunk * S, chunk * A, chunk
+
+    def remote(p, st, src, dst, device):
         return pltpu.make_async_remote_copy(
-            src_ref=wb.at[k, pl.ds(pl.multiple_of(f * part, 16), part), :],
-            dst_ref=w1in.at[k, f_in],
-            send_sem=w_ss.at[k, 0], recv_sem=w_rs.at[k, 0],
-            device_id=(f, sub), device_id_type=MESH)
-
-    def b_copy(k, j, j_in):
-        return pltpu.make_async_remote_copy(
-            src_ref=red.at[k, pl.ds(pl.multiple_of(j * group, 16), group), :],
-            dst_ref=w2in.at[k, j_in],
-            send_sem=w_ss.at[k, 1], recv_sem=w_rs.at[k, 1],
-            device_id=(face, a_id * B + j), device_id_type=MESH)
-
-    def a_copy(k, j, j_in):
-        return pltpu.make_async_remote_copy(
-            src_ref=red2.at[k, pl.ds(pl.multiple_of(j * chunk, 16), chunk), :],
-            dst_ref=w3in.at[k, j_in],
-            send_sem=w_ss.at[k, 2], recv_sem=w_rs.at[k, 2],
-            device_id=(face, j * B + b_id), device_id_type=MESH)
-
-    def spot(k, start, size):
-        return gath.at[k, pl.ds(pl.multiple_of(start, 16), size), :]
-
-    def a_gather(k, j, own):
-        place = spot(k, face * part + b_id * group + own * chunk, chunk)
-        return pltpu.make_async_remote_copy(
-            src_ref=place, dst_ref=place,
-            send_sem=w_ss.at[k, 3], recv_sem=w_rs.at[k, 3],
-            device_id=(face, j * B + b_id), device_id_type=MESH)
-
-    def b_gather(k, j, own):
-        place = spot(k, face * part + own * group, group)
-        return pltpu.make_async_remote_copy(
-            src_ref=place, dst_ref=place,
-            send_sem=w_ss.at[k, 4], recv_sem=w_rs.at[k, 4],
-            device_id=(face, a_id * B + j), device_id_type=MESH)
-
-    def face_gather(k, f, own):
-        place = spot(k, own * part, part)
-        return pltpu.make_async_remote_copy(
-            src_ref=place, dst_ref=place,
-            send_sem=w_ss.at[k, 5], recv_sem=w_rs.at[k, 5],
-            device_id=(f, sub), device_id_type=MESH)
-
-    sizes = ((F - 1) * part, (B - 1) * group, (A - 1) * chunk, (A - 1) * chunk, (B - 1) * group, (F - 1) * part)
-
-    counts = (F - 1, B - 1, A - 1)
-
-    def arrived_all(k, st):
-        if sizes[st]:
-            slots = (w1in, w2in, w3in)
-            take(slots[st].at[k, 0:counts[st]] if st < 3 else gath.at[k, 0:sizes[st], :], w_rs.at[k, st])
-
-    def reduce_start(k):
-        peers(F, face, lambda f: face_copy(k, f, face).start())
-
-    def summed(first, count, mine, ref, k):
+            src_ref=src, dst_ref=dst, send_sem=w_ss.at[p, st], recv_sem=w_rs.at[p, st],
+            device_id=device, device_id_type=MESH)
+
+    def to_face(f):
+        return (f, sub)
+
+    def to_b(j):
+        return (face, a_id * B + j)
+
+    def to_a(j):
+        return (face, j * B + b_id)
+
+    def inner(p, level, start, ref):
+        size = sizes(p)[level]
+        base = starts[p] // D * (D // F, D // (F * B), 1)[level - 1]
+        return ref.at[pl.ds(pl.multiple_of(base + start * size, 16), size), :]
+
+    def face_copy(p, f, f_in):
+        part = sizes(p)[0]
+        return remote(p, 0, spot(wb, p, f * part, part), w1in.at[f_in, whole(p, 0)], to_face(f))
+
+    def b_copy(p, j, j_in):
+        return remote(p, 1, inner(p, 1, j, red), w2in.at[j_in, whole(p, 1)], to_b(j))
+
+    def a_copy(p, j, j_in):
+        return remote(p, 2, inner(p, 2, j, red2), w3in.at[j_in, whole(p, 2)], to_a(j))
+
+    def a_gather(p, j, own):
+        part, group, chunk = sizes(p)
+        place = spot(gath, p, face * part + b_id * group + own * chunk, chunk)
+        return remote(p, 3, place, place, to_a(j))
+
+    def b_gather(p, j, own):
+        part, group, chunk = sizes(p)
+        place = spot(gath, p, face * part + own * group, group)
+        return remote(p, 4, place, place, to_b(j))
+
+    def face_gather(p, f, own):
+        part, group, chunk = sizes(p)
+        place = spot(gath, p, own * part, part)
+        return remote(p, 5, place, place, to_face(f))
+
+    counts = (F - 1, B - 1, A - 1, A - 1, B - 1, F - 1)
+
+    def moved(p, st):
+        return counts[st] * sizes(p)[(0, 1, 2, 2, 1, 0)[st]]
+
+    def arrived_all(p, st):
+        if counts[st]:
+            if st < 3:
+                take((w1in, w2in, w3in)[st].at[0:counts[st], whole(p, st)], w_rs.at[p, st])
+            else:
+                take(gath.at[starts[p]:starts[p] + moved(p, st), :], w_rs.at[p, st])
+
+    def reduce_start(p):
+        peers(F, face, lambda f: face_copy(p, f, face).start())
+
+    def summed(first, count, mine, ref, span):
         def step(d, tot):
-            return tot + ref[k, lax.rem(mine + d, count)].astype(F32)
+            return tot + ref[lax.rem(mine + d, count), span, :].astype(F32)
         return lax.fori_loop(1, count, step, first)
 
-    def reduce_b(k):
-        arrived_all(k, 0)
+    def reduce_b(p):
+        arrived_all(p, 0)
+        part, group, chunk = sizes(p)
+        lo = starts[p] // F
         for r in range(B):
-            at = pl.ds(pl.multiple_of(face * part + r * group, 16), group)
-            tot = wf[k, at, :]
+            tot = wf[pl.ds(pl.multiple_of(starts[p] + face * part + r * group, 16), group), :]
             for f in range(1, F):
-                tot = tot + w1in[k, lax.rem(face + f, F), r * group:(r + 1) * group, :].astype(F32)
-            accf[k, r * group:(r + 1) * group, :] = tot
-            red[k, r * group:(r + 1) * group, :] = tot.astype(BF16)
-        peers(B, b_id, lambda j: b_copy(k, j, b_id).start())
-
-    def reduce_a(k):
-        arrived_all(k, 1)
-        tot = summed(accf[k, pl.ds(pl.multiple_of(b_id * group, 16), group), :], B, b_id, w2in, k)
-        acc2[k] = tot
-        red2[k] = tot.astype(BF16)
-        peers(A, a_id, lambda j: a_copy(k, j, a_id).start())
-
-    def gather_a(k):
-        arrived_all(k, 2)
-        tot = summed(acc2[k, pl.ds(pl.multiple_of(a_id * chunk, 16), chunk), :], A, a_id, w3in, k)
-        own = pl.ds(pl.multiple_of(face * part + b_id * group + a_id * chunk, 16), chunk)
-        gath[k, own, :] = (tot * scale).astype(BF16)
-        peers(A, a_id, lambda j: a_gather(k, j, a_id).start())
-
-    def gather_b(k):
-        arrived_all(k, 3)
-        peers(B, b_id, lambda j: b_gather(k, j, b_id).start())
-
-    def gather_face(k):
-        arrived_all(k, 4)
-        peers(F, face, lambda f: face_gather(k, f, face).start())
-
-    def gather_end(k):
-        arrived_all(k, 5)
-
-    def drain(k):
+                tot = tot + w1in[lax.rem(face + f, F), lo + r * group:lo + (r + 1) * group, :].astype(F32)
+            accf[lo + r * group:lo + (r + 1) * group, :] = tot
+            red[lo + r * group:lo + (r + 1) * group, :] = tot.astype(BF16)
+        peers(B, b_id, lambda j: b_copy(p, j, b_id).start())
+
+    def reduce_a(p):
+        arrived_all(p, 1)
+        part, group, chunk = sizes(p)
+        own = pl.ds(pl.multiple_of(starts[p] // F + b_id * group, 16), group)
+        tot = summed(accf[own, :], B, b_id, w2in, whole(p, 1))
+        acc2[whole(p, 1), :] = tot
+        red2[whole(p, 1), :] = tot.astype(BF16)
+        peers(A, a_id, lambda j: a_copy(p, j, a_id).start())
+
+    def gather_a(p):
+        arrived_all(p, 2)
+        part, group, chunk = sizes(p)
+        own = pl.ds(pl.multiple_of(starts[p] // (F * B) + a_id * chunk, 16), chunk)
+        tot = summed(acc2[own, :], A, a_id, w3in, whole(p, 2))
+        own = pl.ds(pl.multiple_of(starts[p] + face * part + b_id * group + a_id * chunk, 16), chunk)
+        gath[own, :] = (tot * scale).astype(BF16)
+        peers(A, a_id, lambda j: a_gather(p, j, a_id).start())
+
+    def gather_b(p):
+        arrived_all(p, 3)
+        peers(B, b_id, lambda j: b_gather(p, j, b_id).start())
+
+    def gather_face(p):
+        arrived_all(p, 4)
+        peers(F, face, lambda f: face_gather(p, f, face).start())
+
+    def gather_end(p):
+        arrived_all(p, 5)
+
+    def drain(p):
         for st in range(6):
-            if sizes[st]:
-                take((wb, red, red2, gath, gath, gath)[st].at[k, 0:sizes[st], :], w_ss.at[k, st])
-
-    for k in range(2):
-        put(k, 14 * C, jnp.zeros((rows - 14 * C, LANES), F32))
+            if counts[st]:
+                lo = starts[p] // (1, F, F * B, 1, 1, 1)[st]
+                take((wb, red, red2, gath, gath, gath)[st].at[lo:lo + moved(p, st), :], w_ss.at[p, st])
+
+    lines = 14 * C
+    second_at = max(lines + 16, starts[1])
+    used = second_at + lines
+    put(used, jnp.zeros((wf.shape[0] - used, LANES), F32)) if wf.shape[0] > used else None
+    put(lines + 16, jnp.zeros((second_at - lines - 16, LANES), F32)) if second_at > lines + 16 else None
+    early = [p for p in range(len(pieces)) if starts[p] + pieces[p] <= second_at]
+    late = [p for p in range(len(pieces)) if p not in early]
     weight_grad(0, win_in, gs1)
     bias = jnp.sum(jnp.sum(gh, axis=0), axis=0, keepdims=True)
     bias = jnp.concatenate([bias, jnp.zeros((1, 2 * LANES - C), F32)], axis=1)
     line = iota((16, LANES), 0)
-    put(0, 14 * C, jnp.where(line == 0, bias[:, 0:LANES], jnp.where(line == 1, bias[:, LANES:], 0.0)))
-    reduce_start(0)
+    put(lines, jnp.where(line == 0, bias[:, 0:LANES], jnp.where(line == 1, bias[:, LANES:], 0.0)))
+    for p in early:
+        reduce_start(p)
 
     half = (T + 2) // 2 * W
     conv(gs1, w1, pg, 0, half, True)
-    reduce_b(0)
-    conv(gs1, w1, pg, half, MP - half, True)
-    rims = dot(pad_rims, pg[...].astype(BF16)).astype(BF16)
-    ex_start(3, recv_mat, recv_low, rims)
+    for p in early:
+        reduce_b(p)
     halo1 = ex_wait(1, recv_mat, recv_low)
     add_halo(pad_act, halo1)
     windows(pad_act, win_act, T + 2)
-    weight_grad(1, win_act, gs2)
-    reduce_start(1)
+    weight_grad(second_at, win_act, gs2)
+    for p in late:
+        reduce_start(p)
     conv(win_act, w2, second, 0, M // 2, False)
     reduce_b(1)
     reduce_a(0)
     conv(win_act, w2, second, M // 2, M // 2, False)
+    gather_a(0)
+    conv(gs1, w1, pg, half, MP - half, True)
+    rims = dot(pad_rims, pg[...].astype(BF16)).astype(BF16)
+    gact[...] = pg[...].reshape(T + 2, W, C)[1:T + 1]
+    reduce_a(1)
     hi, lo = split(second[...] + pad_in[1:T + 1, 1:W + 1, :].reshape(M, C))
     mean = hot(pool_pos(iota((1, M), 1)) == iota((H * 16, M), 0))
     down = (dot(mean, hi) + dot(mean, lo)) * 0.25
     pooled[...] = down.reshape(H, 16, C)[:, 0:H, :].astype(BF16)
-    gather_a(0)
-    reduce_a(1)
-    gact[...] = pg[...].reshape(T + 2, W, C)[1:T + 1]
+    gather_b(0)
+    gather_a(1)
+    ex_start(3, recv_mat, recv_low, rims)
+    gather_b(1)
+    gather_face(0)
     halo3 = ex_wait(3, send_mat, send_low)
     total = fold(gact, halo3) + gpad2[2:T + 2, 2:T + 2, :]
     gin[...] = total.astype(BF16)
-    gather_b(0)
-    gather_a(1)
-    gather_b(1)
-    gather_face(0)
     gather_face(1)
     gather_end(0)
     gather_end(1)
     for ph in range(4):
         ex_drain(ph)
-    for k in range(2):
-        drain(k)
-
-
-def finish(C, pooled_in, gin_in, gath, pooled, gin, gw1, gb1, gw2):
+    for p in range(len(pieces)):
+        drain(p)
+
+
+def finish(C, second_at, pooled_in, gin_in, gath, pooled, gin, gw1, gb1, gw2):
     pooled[...] = pooled_in[...]
     gin[...] = gin_in[...]
-    for k, out in ((0, gw1), (1, gw2)):
+    for base, out in ((0, gw1), (second_at, gw2)):
         for t in range(9):
-            left = gath[k, t * C:(t + 1) * C, :].astype(F32)
-            pair = gath[k, (9 + t // 2) * C:(10 + t // 2) * C, :].astype(F32)
+            lo = base + t // 2 * 3 * C
+            left = gath[lo + t % 2 * C:lo + t % 2 * C + C, :].astype(F32)
+            lo = lo + (2 * C if t < 8 else C)
+            pair = gath[lo:lo + C, :].astype(F32)
             half = C - LANES
             right = pair[:, 0:half] if t % 2 == 0 else pair[:, half:2 * half]
             out[t // 3, t % 3, :, 0:LANES] = left
             out[t // 3, t % 3, :, LANES:C] = right
-    bias = gath[0, 14 * C:14 * C + 16, :].astype(F32)
+    bias = gath[14 * C:14 * C + 16, :].astype(F32)
     gb1[:, 0:LANES] = bias[0:1]
     gb1[:, LANES:C] = bias[1:2, 0:C - LANES]
 
@@ -443,19 +476,24 @@
     T, C = features.shape[1], features.shape[2]
     H = T // 2
     D = neighbours.shape[0]
-    chunk = -(-(14 * C + 16) // (16 * D)) * 16
+    unit = 16 * D
+    total = -(-(28 * C + 16) // unit)
+    first = (14 * C + 16) // unit
+    rest = total - first
+    units = PIECES if D == 32 else ((first, rest) if first else (1, -(-14 * C // unit)))
+    pieces = tuple(u * unit for u in units)
     A = 4 if S % 4 == 0 else 1
     B = S // A
-    rows, part = chunk * D, chunk * S
+    rows = sum(pieces)
     K = S + 4 * F
     scale = 1.0 / math.sqrt(D * T * T)
     vm = pl.BlockSpec(memory_space=pltpu.VMEM)
     pooled, gin, gath = pl.pallas_call(
-        functools.partial(kernel, S, F, chunk, scale),
+        functools.partial(kernel, S, F, pieces, scale),
         out_shape=(
             pltpu.VMEM((H, H, C), BF16),
             pltpu.VMEM((T, T, C), BF16),
-            pltpu.VMEM((2, rows, LANES), BF16),
+            pltpu.VMEM((rows, LANES), BF16),
         ),
         in_specs=[pl.BlockSpec(memory_space=pl.ANY)] * 7,
         out_specs=(vm,) * 3,
@@ -484,21 +522,21 @@
             pltpu.VMEM((T * W, C), F32),
             pltpu.VMEM(((T + 2) * W, C), F32),
             pltpu.VMEM((T, W, C), F32),
-            pltpu.VMEM((4, K, W + LOW, LANES), BF16),
-            pltpu.VMEM((4, K, W + LOW, LANES), BF16),
-            pltpu.VMEM((2, rows, LANES), F32),
-            pltpu.VMEM((2, rows, LANES), BF16),
-            pltpu.VMEM((2, F, part, LANES), BF16),
-            pltpu.VMEM((2, part, LANES), BF16),
-            pltpu.VMEM((2, part, LANES), F32),
-            pltpu.VMEM((2, B, A * chunk, LANES), BF16),
-            pltpu.VMEM((2, A * chunk, LANES), BF16),
-            pltpu.VMEM((2, A * chunk, LANES), F32),
-            pltpu.VMEM((2, A, chunk, LANES), BF16),
+            pltpu.VMEM((4, K, T + LOW, LANES), BF16),
+            pltpu.VMEM((4, K, T + LOW, LANES), BF16),
+            pltpu.VMEM((rows, LANES), F32),
+            pltpu.VMEM((rows, LANES), BF16),
+            pltpu.VMEM((F, rows // F, LANES), BF16),
+            pltpu.VMEM((rows // F, LANES), BF16),
+            pltpu.VMEM((rows // F, LANES), F32),
+            pltpu.VMEM((B, rows // (F * B), LANES), BF16),
+            pltpu.VMEM((rows // (F * B), LANES), BF16),
+            pltpu.VMEM((rows // (F * B), LANES), F32),
+            pltpu.VMEM((A, rows // D, LANES), BF16),
             pltpu.SemaphoreType.DMA((4,)),
             pltpu.SemaphoreType.DMA((4,)),
-            pltpu.SemaphoreType.DMA((2, 6)),
-            pltpu.SemaphoreType.DMA((2, 6)),
+            pltpu.SemaphoreType.DMA((len(pieces), 6)),
+            pltpu.SemaphoreType.DMA((len(pieces), 6)),
             pltpu.SemaphoreType.DMA((7,)),
         ],
         compiler_params=pltpu.CompilerParams(
@@ -510,7 +548,7 @@
         w_first.reshape(9 * C, C), b_first.reshape(1, C), w_second.reshape(9 * C, C),
     )
     pooled, gin, gw1, gb1, gw2 = pl.pallas_call(
-        functools.partial(finish, C),
+        functools.partial(finish, C, max(14 * C + 16, pieces[0])),
         out_shape=(
             jax.ShapeDtypeStruct((H, H, C), BF16),
             jax.ShapeDtypeStruct((T, T, C), BF16),

time: 54.1 us -> 50.4 us (0.932)
  Pallas kernels: 53.3 us -> 49.6 us
    pallas_call x2, Pallas kernels: 53.3 us -> 49.6 us  [the longest x1 47.5 us: local(): pl.pallas_call(functools.partial(kernel, S, F, pieces, scale), out_shape=...]
where the time goes in v3:
time: 50.4 us; the launch traced here: 50.2 us
  Pallas kernels  49.6 us (98%)
  between operations  0.64 us (1%)
    pallas_call x1, Pallas kernels, local(): pl.pallas_call(functools.partial(kernel, S, F, pieces, scale), out_shape=...  47.5 us
    pallas_call x1, Pallas kernels, local(): pl.pallas_call(functools.partial(finish, C, max(14 * C + 16, pieces[0])),...  2.04 us

profile of v3, /device:TPU:0, one launch (start us, length us, event | category | flops | bytes accessed | tf_op | source)
XLA Modules:
  0.0 50.2 jit_solution(6342843847976640641)
XLA Ops:
  0.6 47.5 %level.1 = (bf16[12,12,192]{2,1,0:T(8,128)(2,1)S(1)}, bf16[24,24,192]{2,1,0:T(8,128)(2,1)S(1)}, bf16[5632,128]{1,0:T(8,128)(2,1)S(1)}) custom-call(s32[4,32]{1,0:T(4,128)} %bitcast.8, s32[4,32]{1,0:T(4,128)} %bitcast.9, bf16[24,24,192]{2,1,0:T(8,128)(2,1)} %feat_hbm.1, bf16[12,12,192]{2,1,0:T(8,128)(2,1)} %cot_hbm.1, bf16[1728,192]{1,0:T(8,128)(2,1)} %bitcast.6, ...), custom_call_target="tpu_custom_call" | custom-call | tf_op jit(solution)/shard_map/level/pallas_call | solution.py:491
  48.2 2.0 %finish.1 = (bf16[12,12,192]{2,1,0:T(8,128)(2,1)}, bf16[24,24,192]{2,1,0:T(8,128)(2,1)}, f32[3,3,192,192]{3,2,1,0:T(8,128)}, f32[1,192]{1,0:T(1,128)}, f32[3,3,192,192]{3,2,1,0:T(8,128)}) custom-call(bf16[12,12,192]{2,1,0:T(8,128)(2,1)S(1)} %get-tuple-element.13.pooled_in, bf16[24,24,192]{2,1,0:T(8,128)(2,1)S(1)} %get-tuple-element.14.gin_in, ...), custom_call_target="tpu_custom_call" | custom-call | tf_op jit(solution)/shard_map/finish/pallas_call | solution.py:550

commit v4 on v3

--- a/solution.py
+++ b/solution.py
@@ -11,7 +11,6 @@
 LANES = 128
 W = 32
 LOW = 16
-PIECES = (5, 6)
 F32, BF16 = jnp.float32, jnp.bfloat16
 MESH = pl.DeviceIdType.MESH
 
@@ -49,13 +48,13 @@
            nbr, rot, feat, cot, w1, b1, w2,
            send_mat, recv_mat, send_low, recv_low, pad_in, pad_act, gpad1, gpad2, cotp,
            win_in, win_act, gs1, gs2, hidden, second, pg, gact,
-           ex_out, ex_in, wf, wb, w1in, red, accf, w2in, red2, acc2, w3in,
+           ex_out, ex_in, wf, wb, w1in, red, accf, w2in, red2, w3in,
            ex_ss, ex_rs, w_ss, w_rs, in_sem):
     T, C = feat.shape[0], feat.shape[2]
     H = T // 2
     face, sub = lax.axis_index("face"), lax.axis_index("sub")
     me = face * S + sub
-    A = 4 if S % 4 == 0 else 1
+    A = 2 if S % 2 == 0 else 1
     B = S // A
     a_id, b_id = sub // B, lax.rem(sub, B)
     M, MP = T * W, (T + 2) * W
@@ -66,16 +65,16 @@
             return c
         lax.fori_loop(1, count, step, 0)
 
+    def load(i):
+        pairs = ((nbr_hbm, nbr), (rot_hbm, rot), (feat_hbm, feat), (w2_hbm, w2), (cot_hbm, cot), (w1_hbm, w1), (b1_hbm, b1))
+        return pltpu.make_async_copy(pairs[i][0], pairs[i][1], in_sem.at[i])
+
+    for i in (2, 0, 1, 3, 4, 5, 6):
+        load(i).start()
+
     barrier = pltpu.get_barrier_semaphore()
     peers(S, sub, lambda j: pl.semaphore_signal(barrier, inc=1, device_id=(face, j), device_id_type=MESH))
     peers(F, face, lambda f: pl.semaphore_signal(barrier, inc=1, device_id=(f, sub), device_id_type=MESH))
-
-    def load(i):
-        pairs = ((nbr_hbm, nbr), (rot_hbm, rot), (feat_hbm, feat), (w2_hbm, w2), (cot_hbm, cot), (w1_hbm, w1), (b1_hbm, b1))
-        return pltpu.make_async_copy(pairs[i][0], pairs[i][1], in_sem.at[i])
-
-    for i in (2, 0, 1, 3, 4, 5, 6):
-        load(i).start()
 
     p32 = iota((W, 4 * W), 0)
     c32 = iota((W, 4 * W), 1)
@@ -174,7 +173,6 @@
     def ex_drain(ph):
         take(ex_out.at[ph, 0:ex_count], ex_ss.at[ph])
 
-    own_rims = hot(iota((4 * W, M), 1) == rim_pos(iota((4 * W, 1), 0), T, 0))
 
     def windows(src, dst, rows):
         for b in range(3):
@@ -199,7 +197,7 @@
         wf[r:r + v.shape[0], :] = v
         wb[r:r + v.shape[0], :] = v.astype(BF16)
 
-    def weight_grad(base, win, gs):
+    def weight_grad(base, win, gs, spare):
         for t in range(9):
             a, b = t // 3, t % 3
             v = dot(win[b], gs[2, (2 - a) * W:(2 - a) * W + MP, :], 0, 0)
@@ -211,17 +209,18 @@
             if t % 2 == 1:
                 put(at + 2 * C, jnp.concatenate([even, rest], axis=1))
             if t == 8:
-                put(at + C, jnp.concatenate([rest, rest], axis=1))
+                put(at + C, jnp.concatenate([rest, spare], axis=1))
 
     pad_in[...] = jnp.zeros(pad_in.shape, F32)
+    load(0).wait()
+    load(1).wait()
+    lax.fori_loop(0, S, send_in_face, 0)
+    lax.fori_loop(0, F, send_cross, 0)
+    own_rims = hot(iota((4 * W, M), 1) == rim_pos(iota((4 * W, 1), 0), T, 0))
     load(2).wait()
     pad_in[1:T + 1, 1:T + 1, :] = feat[...].astype(F32)
     flat_in = pad_in[1:T + 1, 1:W + 1, :].reshape(M, C)
     rims = dot(own_rims, flat_in.astype(BF16)).astype(BF16)
-    load(0).wait()
-    load(1).wait()
-    lax.fori_loop(0, S, send_in_face, 0)
-    lax.fori_loop(0, F, send_cross, 0)
     pl.semaphore_wait(barrier, S + F - 2)
     ex_start(0, send_mat, send_low, rims)
 
@@ -277,16 +276,14 @@
     starts = [sum(pieces[:p]) for p in range(len(pieces))]
 
     def whole(p, level):
-        share = (D // F, D // (F * B), 1)[level]
-        lo = starts[p] // D * share
-        return slice(lo, lo + pieces[p] // D * share)
+        share = F if level == 0 else F * B
+        return slice(starts[p] // share, (starts[p] + pieces[p]) // share)
 
     def spot(ref, p, start, size):
         return ref.at[pl.ds(pl.multiple_of(starts[p] + start, 16), size), :]
 
     def sizes(p):
-        chunk = pieces[p] // D
-        return chunk * S, chunk * A, chunk
+        return pieces[p] // F, pieces[p] // (F * B)
 
     def remote(p, st, src, dst, device):
         return pltpu.make_async_remote_copy(
@@ -302,40 +299,32 @@
     def to_a(j):
         return (face, j * B + b_id)
 
-    def inner(p, level, start, ref):
-        size = sizes(p)[level]
-        base = starts[p] // D * (D // F, D // (F * B), 1)[level - 1]
-        return ref.at[pl.ds(pl.multiple_of(base + start * size, 16), size), :]
-
     def face_copy(p, f, f_in):
         part = sizes(p)[0]
         return remote(p, 0, spot(wb, p, f * part, part), w1in.at[f_in, whole(p, 0)], to_face(f))
 
     def b_copy(p, j, j_in):
-        return remote(p, 1, inner(p, 1, j, red), w2in.at[j_in, whole(p, 1)], to_b(j))
+        group = sizes(p)[1]
+        at = pl.ds(pl.multiple_of(starts[p] // F + j * group, 16), group)
+        return remote(p, 1, red.at[at, :], w2in.at[j_in, whole(p, 1)], to_b(j))
 
     def a_copy(p, j, j_in):
-        return remote(p, 2, inner(p, 2, j, red2), w3in.at[j_in, whole(p, 2)], to_a(j))
-
-    def a_gather(p, j, own):
-        part, group, chunk = sizes(p)
-        place = spot(gath, p, face * part + b_id * group + own * chunk, chunk)
-        return remote(p, 3, place, place, to_a(j))
+        return remote(p, 2, red2.at[whole(p, 1)], w3in.at[j_in, whole(p, 1)], to_a(j))
 
     def b_gather(p, j, own):
-        part, group, chunk = sizes(p)
+        part, group = sizes(p)
         place = spot(gath, p, face * part + own * group, group)
-        return remote(p, 4, place, place, to_b(j))
+        return remote(p, 3, place, place, to_b(j))
 
     def face_gather(p, f, own):
-        part, group, chunk = sizes(p)
+        part = sizes(p)[0]
         place = spot(gath, p, own * part, part)
-        return remote(p, 5, place, place, to_face(f))
-
-    counts = (F - 1, B - 1, A - 1, A - 1, B - 1, F - 1)
+        return remote(p, 4, place, place, to_face(f))
+
+    counts = (F - 1, B - 1, A - 1, B - 1, F - 1)
 
     def moved(p, st):
-        return counts[st] * sizes(p)[(0, 1, 2, 2, 1, 0)[st]]
+        return counts[st] * sizes(p)[(0, 1, 1, 1, 0)[st]]
 
     def arrived_all(p, st):
         if counts[st]:
@@ -354,7 +343,7 @@
 
     def reduce_b(p):
         arrived_all(p, 0)
-        part, group, chunk = sizes(p)
+        part, group = sizes(p)
         lo = starts[p] // F
         for r in range(B):
             tot = wf[pl.ds(pl.multiple_of(starts[p] + face * part + r * group, 16), group), :]
@@ -366,85 +355,80 @@
 
     def reduce_a(p):
         arrived_all(p, 1)
-        part, group, chunk = sizes(p)
+        group = sizes(p)[1]
         own = pl.ds(pl.multiple_of(starts[p] // F + b_id * group, 16), group)
         tot = summed(accf[own, :], B, b_id, w2in, whole(p, 1))
-        acc2[whole(p, 1), :] = tot
         red2[whole(p, 1), :] = tot.astype(BF16)
         peers(A, a_id, lambda j: a_copy(p, j, a_id).start())
 
-    def gather_a(p):
+    def gather_b(p):
         arrived_all(p, 2)
-        part, group, chunk = sizes(p)
-        own = pl.ds(pl.multiple_of(starts[p] // (F * B) + a_id * chunk, 16), chunk)
-        tot = summed(acc2[own, :], A, a_id, w3in, whole(p, 2))
-        own = pl.ds(pl.multiple_of(starts[p] + face * part + b_id * group + a_id * chunk, 16), chunk)
+        part, group = sizes(p)
+        tot = summed(red2[whole(p, 1), :].astype(F32), A, a_id, w3in, whole(p, 1))
+        own = pl.ds(pl.multiple_of(starts[p] + face * part + b_id * group, 16), group)
         gath[own, :] = (tot * scale).astype(BF16)
-        peers(A, a_id, lambda j: a_gather(p, j, a_id).start())
-
-    def gather_b(p):
+        peers(B, b_id, lambda j: b_gather(p, j, b_id).start())
+
+    def gather_face(p):
         arrived_all(p, 3)
-        peers(B, b_id, lambda j: b_gather(p, j, b_id).start())
-
-    def gather_face(p):
+        peers(F, face, lambda f: face_gather(p, f, face).start())
+
+    def gather_end(p):
         arrived_all(p, 4)
-        peers(F, face, lambda f: face_gather(p, f, face).start())
-
-    def gather_end(p):
-        arrived_all(p, 5)
 
     def drain(p):
-        for st in range(6):
+        for st in range(5):
             if counts[st]:
-                lo = starts[p] // (1, F, F * B, 1, 1, 1)[st]
-                take((wb, red, red2, gath, gath, gath)[st].at[lo:lo + moved(p, st), :], w_ss.at[p, st])
+                lo = starts[p] // (1, F, F * B, 1, 1)[st]
+                take((wb, red, red2, gath, gath)[st].at[lo:lo + moved(p, st), :], w_ss.at[p, st])
 
     lines = 14 * C
-    second_at = max(lines + 16, starts[1])
+    second_at = max(lines, starts[1])
     used = second_at + lines
-    put(used, jnp.zeros((wf.shape[0] - used, LANES), F32)) if wf.shape[0] > used else None
-    put(lines + 16, jnp.zeros((second_at - lines - 16, LANES), F32)) if second_at > lines + 16 else None
+    if wf.shape[0] > used:
+        put(used, jnp.zeros((wf.shape[0] - used, LANES), F32))
+    if second_at > lines:
+        put(lines, jnp.zeros((second_at - lines, LANES), F32))
     early = [p for p in range(len(pieces)) if starts[p] + pieces[p] <= second_at]
     late = [p for p in range(len(pieces)) if p not in early]
-    weight_grad(0, win_in, gs1)
     bias = jnp.sum(jnp.sum(gh, axis=0), axis=0, keepdims=True)
-    bias = jnp.concatenate([bias, jnp.zeros((1, 2 * LANES - C), F32)], axis=1)
-    line = iota((16, LANES), 0)
-    put(lines, jnp.where(line == 0, bias[:, 0:LANES], jnp.where(line == 1, bias[:, LANES:], 0.0)))
+    line = iota((C, R), 0)
+    blank = jnp.zeros((C, R), F32)
+    spare = blank
+    for q in range(C // R):
+        spare = jnp.where(line == q, bias[:, q * R:(q + 1) * R], spare)
+    weight_grad(0, win_in, gs1, spare)
     for p in early:
         reduce_start(p)
 
     half = (T + 2) // 2 * W
     conv(gs1, w1, pg, 0, half, True)
-    for p in early:
-        reduce_b(p)
+    reduce_b(0)
+    conv(gs1, w1, pg, half, MP - half, True)
+    rims = dot(pad_rims, pg[...].astype(BF16)).astype(BF16)
+    gact[...] = pg[...].reshape(T + 2, W, C)[1:T + 1]
+    ex_start(3, recv_mat, recv_low, rims)
     halo1 = ex_wait(1, recv_mat, recv_low)
     add_halo(pad_act, halo1)
     windows(pad_act, win_act, T + 2)
-    weight_grad(second_at, win_act, gs2)
+    weight_grad(second_at, win_act, gs2, blank)
     for p in late:
         reduce_start(p)
     conv(win_act, w2, second, 0, M // 2, False)
     reduce_b(1)
+    conv(win_act, w2, second, M // 2, M // 2, False)
     reduce_a(0)
-    conv(win_act, w2, second, M // 2, M // 2, False)
-    gather_a(0)
-    conv(gs1, w1, pg, half, MP - half, True)
-    rims = dot(pad_rims, pg[...].astype(BF16)).astype(BF16)
-    gact[...] = pg[...].reshape(T + 2, W, C)[1:T + 1]
-    reduce_a(1)
     hi, lo = split(second[...] + pad_in[1:T + 1, 1:W + 1, :].reshape(M, C))
     mean = hot(pool_pos(iota((1, M), 1)) == iota((H * 16, M), 0))
     down = (dot(mean, hi) + dot(mean, lo)) * 0.25
     pooled[...] = down.reshape(H, 16, C)[:, 0:H, :].astype(BF16)
     gather_b(0)
-    gather_a(1)
-    ex_start(3, recv_mat, recv_low, rims)
-    gather_b(1)
-    gather_face(0)
     halo3 = ex_wait(3, send_mat, send_low)
     total = fold(gact, halo3) + gpad2[2:T + 2, 2:T + 2, :]
     gin[...] = total.astype(BF16)
+    reduce_a(1)
+    gather_b(1)
+    gather_face(0)
     gather_face(1)
     gather_end(0)
     gather_end(1)
@@ -454,36 +438,48 @@
         drain(p)
 
 
-def finish(C, second_at, pooled_in, gin_in, gath, pooled, gin, gw1, gb1, gw2):
-    pooled[...] = pooled_in[...]
-    gin[...] = gin_in[...]
-    for base, out in ((0, gw1), (second_at, gw2)):
+def finish(C, second_at, pooled_in, gin_in, gath, pooled, gin, gw1, gb1, gw2, wide, bias_row, sem):
+    def out(i, src, dst):
+        return pltpu.make_async_copy(src, dst, sem.at[i])
+
+    copies = [out(0, pooled_in, pooled), out(1, gin_in, gin)]
+    for c in copies:
+        c.start()
+    half = C - LANES
+    for k, (base, dst) in enumerate(((0, gw1), (second_at, gw2))):
         for t in range(9):
             lo = base + t // 2 * 3 * C
             left = gath[lo + t % 2 * C:lo + t % 2 * C + C, :].astype(F32)
             lo = lo + (2 * C if t < 8 else C)
             pair = gath[lo:lo + C, :].astype(F32)
-            half = C - LANES
             right = pair[:, 0:half] if t % 2 == 0 else pair[:, half:2 * half]
-            out[t // 3, t % 3, :, 0:LANES] = left
-            out[t // 3, t % 3, :, LANES:C] = right
-    bias = gath[14 * C:14 * C + 16, :].astype(F32)
-    gb1[:, 0:LANES] = bias[0:1]
-    gb1[:, LANES:C] = bias[1:2, 0:C - LANES]
+            wide[k, t // 3, t % 3, :, 0:LANES] = left
+            wide[k, t // 3, t % 3, :, LANES:C] = right
+            if t % 3 == 2:
+                copies.append(out(2 + 3 * k + t // 3, wide.at[k, t // 3], dst.at[t // 3]))
+                copies[-1].start()
+    bias = gath[13 * C:13 * C + 16, :].astype(F32)
+    for q in range(C // half):
+        bias_row[:, q * half:(q + 1) * half] = bias[q:q + 1, half:2 * half]
+    copies.append(out(8, bias_row, gb1))
+    copies[-1].start()
+    for c in copies:
+        c.wait()
 
 
 def local(S, F, features, w_first, b_first, w_second, neighbours, rotations, cotangent):
     T, C = features.shape[1], features.shape[2]
     H = T // 2
     D = neighbours.shape[0]
-    unit = 16 * D
-    total = -(-(28 * C + 16) // unit)
-    first = (14 * C + 16) // unit
-    rest = total - first
-    units = PIECES if D == 32 else ((first, rest) if first else (1, -(-14 * C // unit)))
+    A = 2 if S % 2 == 0 else 1
+    B = S // A
+    unit = 16 * F * B
+    first = 14 * C // unit
+    if first:
+        units = (first, -(-28 * C // unit) - first)
+    else:
+        units = (1, -(-14 * C // unit))
     pieces = tuple(u * unit for u in units)
-    A = 4 if S % 4 == 0 else 1
-    B = S // A
     rows = sum(pieces)
     K = S + 4 * F
     scale = 1.0 / math.sqrt(D * T * T)
@@ -531,12 +527,11 @@
             pltpu.VMEM((rows // F, LANES), F32),
             pltpu.VMEM((B, rows // (F * B), LANES), BF16),
             pltpu.VMEM((rows // (F * B), LANES), BF16),
-            pltpu.VMEM((rows // (F * B), LANES), F32),
-            pltpu.VMEM((A, rows // D, LANES), BF16),
+            pltpu.VMEM((A, rows // (F * B), LANES), BF16),
             pltpu.SemaphoreType.DMA((4,)),
             pltpu.SemaphoreType.DMA((4,)),
-            pltpu.SemaphoreType.DMA((len(pieces), 6)),
-            pltpu.SemaphoreType.DMA((len(pieces), 6)),
+            pltpu.SemaphoreType.DMA((len(pieces), 5)),
+            pltpu.SemaphoreType.DMA((len(pieces), 5)),
             pltpu.SemaphoreType.DMA((7,)),
         ],
         compiler_params=pltpu.CompilerParams(
@@ -548,7 +543,7 @@
         w_first.reshape(9 * C, C), b_first.reshape(1, C), w_second.reshape(9 * C, C),
     )
     pooled, gin, gw1, gb1, gw2 = pl.pallas_call(
-        functools.partial(finish, C, max(14 * C + 16, pieces[0])),
+        functools.partial(finish, C, max(14 * C, pieces[0])),
         out_shape=(
             jax.ShapeDtypeStruct((H, H, C), BF16),
             jax.ShapeDtypeStruct((T, T, C), BF16),
@@ -557,7 +552,12 @@
             jax.ShapeDtypeStruct((3, 3, C, C), F32),
         ),
         in_specs=[vm] * 3,
-        out_specs=(vm,) * 5,
+        out_specs=(pl.BlockSpec(memory_space=pl.ANY),) * 5,
+        scratch_shapes=[
+            pltpu.VMEM((2, 3, 3, C, C), F32),
+            pltpu.VMEM((1, C), F32),
+            pltpu.SemaphoreType.DMA((9,)),
+        ],
         compiler_params=pltpu.CompilerParams(vmem_limit_bytes=24 * 1024 * 1024),
         name="finish",
     )(pooled, gin, gath)

time: 50.4 us -> 48.3 us (0.958)
  Pallas kernels: 49.6 us -> 47.5 us
    pallas_call x1, Pallas kernels: 47.5 us -> 45.5 us  [local(): pl.pallas_call(functools.partial(kernel, S, F, pieces, scale), out_shape=...]
where the time goes in v4:
time: 48.3 us; the launch traced here: 48.1 us
  Pallas kernels  47.5 us (98%)
  between operations  0.64 us (1%)
    pallas_call x1, Pallas kernels, local(): pl.pallas_call(functools.partial(kernel, S, F, pieces, scale), out_shape=...  45.5 us
    pallas_call x1, Pallas kernels, local(): pl.pallas_call(functools.partial(finish, C, max(14 * C, pieces[0])), out_...  2 us

profile of v4, /device:TPU:0, one launch (start us, length us, event | category | flops | bytes accessed | tf_op | source)
XLA Modules:
  0.0 48.1 jit_solution(8614687913565437306)
XLA Ops:
  0.6 45.5 %level.1 = (bf16[12,12,192]{2,1,0:T(8,128)(2,1)S(1)}, bf16[24,24,192]{2,1,0:T(8,128)(2,1)S(1)}, bf16[5376,128]{1,0:T(8,128)(2,1)S(1)}) custom-call(s32[4,32]{1,0:T(4,128)} %bitcast.8, s32[4,32]{1,0:T(4,128)} %bitcast.9, bf16[24,24,192]{2,1,0:T(8,128)(2,1)} %feat_hbm.1, bf16[12,12,192]{2,1,0:T(8,128)(2,1)} %cot_hbm.1, bf16[1728,192]{1,0:T(8,128)(2,1)} %bitcast.6, ...), custom_call_target="tpu_custom_call" | custom-call | tf_op jit(solution)/shard_map/level/pallas_call | solution.py:487
  46.1 2.0 %finish.1 = (bf16[12,12,192]{2,1,0:T(8,128)(2,1)}, bf16[24,24,192]{2,1,0:T(8,128)(2,1)}, f32[3,3,192,192]{3,2,1,0:T(8,128)}, f32[1,192]{1,0:T(1,128)}, f32[3,3,192,192]{3,2,1,0:T(8,128)}) custom-call(bf16[12,12,192]{2,1,0:T(8,128)(2,1)S(1)} %get-tuple-element.13.pooled_in, bf16[24,24,192]{2,1,0:T(8,128)(2,1)S(1)} %get-tuple-element.14.gin_in, ...), custom_call_target="tpu_custom_call" | custom-call | tf_op jit(solution)/shard_map/finish/pallas_call | solution.py:545

commit v5 on v4

--- a/solution.py
+++ b/solution.py
@@ -155,7 +155,10 @@
         bottom = dot(low[...], wide).reshape(slots, LOW, LANES)
         ex_out[ph] = jnp.concatenate([top, bottom], axis=1).astype(BF16)
         peers(F, face, lambda f: ex_face(ph, f, face).start())
-        peers(S, sub, lambda j: ex_sub(ph, j, sub).start())
+        def step(d, c):
+            ex_sub(ph, lax.rem(sub + S - d, S), sub).start()
+            return c
+        lax.fori_loop(1, S, step, 0)
 
     def take(ref, sem):
         pltpu.make_async_copy(ref, ref, sem).wait()
@@ -404,10 +407,6 @@
     half = (T + 2) // 2 * W
     conv(gs1, w1, pg, 0, half, True)
     reduce_b(0)
-    conv(gs1, w1, pg, half, MP - half, True)
-    rims = dot(pad_rims, pg[...].astype(BF16)).astype(BF16)
-    gact[...] = pg[...].reshape(T + 2, W, C)[1:T + 1]
-    ex_start(3, recv_mat, recv_low, rims)
     halo1 = ex_wait(1, recv_mat, recv_low)
     add_halo(pad_act, halo1)
     windows(pad_act, win_act, T + 2)
@@ -416,18 +415,22 @@
         reduce_start(p)
     conv(win_act, w2, second, 0, M // 2, False)
     reduce_b(1)
+    conv(gs1, w1, pg, half, MP - half, True)
+    rims = dot(pad_rims, pg[...].astype(BF16)).astype(BF16)
+    gact[...] = pg[...].reshape(T + 2, W, C)[1:T + 1]
+    reduce_a(0)
+    ex_start(3, recv_mat, recv_low, rims)
     conv(win_act, w2, second, M // 2, M // 2, False)
-    reduce_a(0)
     hi, lo = split(second[...] + pad_in[1:T + 1, 1:W + 1, :].reshape(M, C))
     mean = hot(pool_pos(iota((1, M), 1)) == iota((H * 16, M), 0))
     down = (dot(mean, hi) + dot(mean, lo)) * 0.25
     pooled[...] = down.reshape(H, 16, C)[:, 0:H, :].astype(BF16)
+    reduce_a(1)
     gather_b(0)
+    gather_b(1)
     halo3 = ex_wait(3, send_mat, send_low)
     total = fold(gact, halo3) + gpad2[2:T + 2, 2:T + 2, :]
     gin[...] = total.astype(BF16)
-    reduce_a(1)
-    gather_b(1)
     gather_face(0)
     gather_face(1)
     gather_end(0)

time: 48.3 us -> 46.6 us (0.965)
  Pallas kernels: 47.5 us -> 45.8 us
    pallas_call x1, Pallas kernels: 45.5 us -> 43.9 us  [local(): pl.pallas_call(functools.partial(kernel, S, F, pieces, scale), out_shape=...]
where the time goes in v5:
time: 46.6 us; the launch traced here: 46.5 us
  Pallas kernels  45.8 us (98%)
  between operations  0.64 us (1%)
    pallas_call x1, Pallas kernels, local(): pl.pallas_call(functools.partial(kernel, S, F, pieces, scale), out_shape=...  43.9 us
    pallas_call x1, Pallas kernels, local(): pl.pallas_call(functools.partial(finish, C, max(14 * C, pieces[0])), out_...  2 us

profile of v5, /device:TPU:0, one launch (start us, length us, event | category | flops | bytes accessed | tf_op | source)
XLA Modules:
  0.0 46.5 jit_solution(1242866128174130352)
XLA Ops:
  0.6 43.9 %level.1 = (bf16[12,12,192]{2,1,0:T(8,128)(2,1)S(1)}, bf16[24,24,192]{2,1,0:T(8,128)(2,1)S(1)}, bf16[5376,128]{1,0:T(8,128)(2,1)S(1)}) custom-call(s32[4,32]{1,0:T(4,128)} %bitcast.8, s32[4,32]{1,0:T(4,128)} %bitcast.9, bf16[24,24,192]{2,1,0:T(8,128)(2,1)} %feat_hbm.1, bf16[12,12,192]{2,1,0:T(8,128)(2,1)} %cot_hbm.1, bf16[1728,192]{1,0:T(8,128)(2,1)} %bitcast.6, ...), custom_call_target="tpu_custom_call" | custom-call | tf_op jit(solution)/shard_map/level/pallas_call | solution.py:490
  44.5 2.0 %finish.1 = (bf16[12,12,192]{2,1,0:T(8,128)(2,1)}, bf16[24,24,192]{2,1,0:T(8,128)(2,1)}, f32[3,3,192,192]{3,2,1,0:T(8,128)}, f32[1,192]{1,0:T(1,128)}, f32[3,3,192,192]{3,2,1,0:T(8,128)}) custom-call(bf16[12,12,192]{2,1,0:T(8,128)(2,1)S(1)} %get-tuple-element.13.pooled_in, bf16[24,24,192]{2,1,0:T(8,128)(2,1)S(1)} %get-tuple-element.14.gin_in, ...), custom_call_target="tpu_custom_call" | custom-call | tf_op jit(solution)/shard_map/finish/pallas_call | solution.py:548

commit v6 on v5

--- a/solution.py
+++ b/solution.py
@@ -134,13 +134,13 @@
     def ex_sub(ph, j, s_in):
         return pltpu.make_async_remote_copy(
             src_ref=ex_out.at[ph, j], dst_ref=ex_in.at[ph, s_in],
-            send_sem=ex_ss.at[ph], recv_sem=ex_rs.at[ph],
+            send_sem=ex_ss.at[0], recv_sem=ex_rs.at[ph],
             device_id=(face, j), device_id_type=MESH)
 
     def ex_face(ph, f, f_in):
         return pltpu.make_async_remote_copy(
             src_ref=ex_out.at[ph, pl.ds(S + 4 * f, 4)], dst_ref=ex_in.at[ph, pl.ds(S + 4 * f_in, 4)],
-            send_sem=ex_ss.at[ph], recv_sem=ex_rs.at[ph],
+            send_sem=ex_ss.at[0], recv_sem=ex_rs.at[ph],
             device_id=(f, sub), device_id_type=MESH)
 
     slots = S + 4 * F
@@ -173,8 +173,8 @@
         rest = rest[0:4 * W, 0:R] + rest[4 * W:8 * W, R:2 * R]
         return jnp.concatenate([left, rest], axis=1)
 
-    def ex_drain(ph):
-        take(ex_out.at[ph, 0:ex_count], ex_ss.at[ph])
+    def ex_drain():
+        take(ex_out.at[:, 0:ex_count], ex_ss.at[0])
 
 
     def windows(src, dst, rows):
@@ -290,7 +290,7 @@
 
     def remote(p, st, src, dst, device):
         return pltpu.make_async_remote_copy(
-            src_ref=src, dst_ref=dst, send_sem=w_ss.at[p, st], recv_sem=w_rs.at[p, st],
+            src_ref=src, dst_ref=dst, send_sem=w_ss.at[0], recv_sem=w_rs.at[p, st],
             device_id=device, device_id_type=MESH)
 
     def to_face(f):
@@ -379,11 +379,9 @@
     def gather_end(p):
         arrived_all(p, 4)
 
-    def drain(p):
-        for st in range(5):
-            if counts[st]:
-                lo = starts[p] // (1, F, F * B, 1, 1)[st]
-                take((wb, red, red2, gath, gath)[st].at[lo:lo + moved(p, st), :], w_ss.at[p, st])
+    def drain():
+        sent = sum(moved(p, st) for p in range(len(pieces)) for st in range(5))
+        take(wf.at[0:sent // 2, :], w_ss.at[0])
 
     lines = 14 * C
     second_at = max(lines, starts[1])
@@ -415,12 +413,12 @@
         reduce_start(p)
     conv(win_act, w2, second, 0, M // 2, False)
     reduce_b(1)
+    conv(win_act, w2, second, M // 2, M // 2, False)
+    reduce_a(0)
     conv(gs1, w1, pg, half, MP - half, True)
     rims = dot(pad_rims, pg[...].astype(BF16)).astype(BF16)
     gact[...] = pg[...].reshape(T + 2, W, C)[1:T + 1]
-    reduce_a(0)
     ex_start(3, recv_mat, recv_low, rims)
-    conv(win_act, w2, second, M // 2, M // 2, False)
     hi, lo = split(second[...] + pad_in[1:T + 1, 1:W + 1, :].reshape(M, C))
     mean = hot(pool_pos(iota((1, M), 1)) == iota((H * 16, M), 0))
     down = (dot(mean, hi) + dot(mean, lo)) * 0.25
@@ -435,10 +433,8 @@
     gather_face(1)
     gather_end(0)
     gather_end(1)
-    for ph in range(4):
-        ex_drain(ph)
-    for p in range(len(pieces)):
-        drain(p)
+    ex_drain()
+    drain()
 
 
 def finish(C, second_at, pooled_in, gin_in, gath, pooled, gin, gw1, gb1, gw2, wide, bias_row, sem):
@@ -458,15 +454,16 @@
             right = pair[:, 0:half] if t % 2 == 0 else pair[:, half:2 * half]
             wide[k, t // 3, t % 3, :, 0:LANES] = left
             wide[k, t // 3, t % 3, :, LANES:C] = right
-            if t % 3 == 2:
-                copies.append(out(2 + 3 * k + t // 3, wide.at[k, t // 3], dst.at[t // 3]))
-                copies[-1].start()
+            copies.append(out(2 + k, wide.at[k, t // 3, t % 3], dst.at[t // 3, t % 3]))
+            copies[-1].start()
     bias = gath[13 * C:13 * C + 16, :].astype(F32)
     for q in range(C // half):
         bias_row[:, q * half:(q + 1) * half] = bias[q:q + 1, half:2 * half]
-    copies.append(out(8, bias_row, gb1))
+    copies.append(out(4, bias_row, gb1))
     copies[-1].start()
-    for c in copies:
+    for k, dst in enumerate((gw1, gw2)):
+        out(2 + k, wide.at[k], dst).wait()
+    for c in copies[:2] + copies[-1:]:
         c.wait()
 
 
@@ -531,9 +528,9 @@
             pltpu.VMEM((B, rows // (F * B), LANES), BF16),
             pltpu.VMEM((rows // (F * B), LANES), BF16),
             pltpu.VMEM((A, rows // (F * B), LANES), BF16),
+            pltpu.SemaphoreType.DMA((1,)),
             pltpu.SemaphoreType.DMA((4,)),
-            pltpu.SemaphoreType.DMA((4,)),
-            pltpu.SemaphoreType.DMA((len(pieces), 5)),
+            pltpu.SemaphoreType.DMA((1,)),
             pltpu.SemaphoreType.DMA((len(pieces), 5)),
             pltpu.SemaphoreType.DMA((7,)),
         ],
@@ -559,7 +556,7 @@
         scratch_shapes=[
             pltpu.VMEM((2, 3, 3, C, C), F32),
             pltpu.VMEM((1, C), F32),
-            pltpu.SemaphoreType.DMA((9,)),
+            pltpu.SemaphoreType.DMA((5,)),
         ],
         compiler_params=pltpu.CompilerParams(vmem_limit_bytes=24 * 1024 * 1024),
         name="finish",

time: 46.6 us -> 46.6 us (level)
  no operation moved by 1% of the time
where the time goes in v6:
time: 46.6 us; the launch traced here: 46.5 us
  Pallas kernels  45.8 us (98%)
  between operations  0.64 us (1%)
    pallas_call x1, Pallas kernels, local(): pl.pallas_call(functools.partial(kernel, S, F, pieces, scale), out_shape=...  43.9 us
    pallas_call x1, Pallas kernels, local(): pl.pallas_call(functools.partial(finish, C, max(14 * C, pieces[0])), out_...  1.95 us

profile of v6, /device:TPU:0, one launch (start us, length us, event | category | flops | bytes accessed | tf_op | source)
XLA Modules:
  0.0 46.5 jit_solution(15076023644883711100)
XLA Ops:
  0.6 43.9 %level.1 = (bf16[12,12,192]{2,1,0:T(8,128)(2,1)S(1)}, bf16[24,24,192]{2,1,0:T(8,128)(2,1)S(1)}, bf16[5376,128]{1,0:T(8,128)(2,1)S(1)}) custom-call(s32[4,32]{1,0:T(4,128)} %bitcast.8, s32[4,32]{1,0:T(4,128)} %bitcast.9, bf16[24,24,192]{2,1,0:T(8,128)(2,1)} %feat_hbm.1, bf16[12,12,192]{2,1,0:T(8,128)(2,1)} %cot_hbm.1, bf16[1728,192]{1,0:T(8,128)(2,1)} %bitcast.6, ...), custom_call_target="tpu_custom_call" | custom-call | tf_op jit(solution)/shard_map/level/pallas_call | solution.py:487
  44.5 1.9 %finish.1 = (bf16[12,12,192]{2,1,0:T(8,128)(2,1)}, bf16[24,24,192]{2,1,0:T(8,128)(2,1)}, f32[3,3,192,192]{3,2,1,0:T(8,128)}, f32[1,192]{1,0:T(1,128)}, f32[3,3,192,192]{3,2,1,0:T(8,128)}) custom-call(bf16[12,12,192]{2,1,0:T(8,128)(2,1)S(1)} %get-tuple-element.13.pooled_in, bf16[24,24,192]{2,1,0:T(8,128)(2,1)S(1)} %get-tuple-element.14.gin_in, ...), custom_call_target="tpu_custom_call" | custom-call | tf_op jit(solution)/shard_map/finish/pallas_call | solution.py:545
